TPU v7x, 128 devices: a whole 4x4x4 slice. The times are simulated.
128 devices in a mesh: dp: 16 (over z, y), tensor: 8 (over x, core).
Axes of the slice: x: 4, y: 4, z: 4, core: 2. Of those that a mesh axis runs over, the one named last changes fastest.
Arguments:
- tokens: bfloat16 [6144, 6144], P('dp'), may hold values from -6 to 6
- grad_out: bfloat16 [6144, 6144], P('dp'), may hold values from -6 to 6
- gate_weight: bfloat16 [96, 12, 128, 128], P('tensor'), may hold values from -0.15625 to 0.15625
- up_weight: bfloat16 [96, 12, 128, 128], P('tensor'), may hold values from -0.15625 to 0.15625
- down_weight: bfloat16 [96, 12, 128, 128], P('tensor'), may hold values from -0.109375 to 0.109375
- gate_index: int32 [96, 12], P('tensor'), may hold values from 0 to 47, as said below
- up_index: int32 [96, 12], P('tensor'), may hold values from 0 to 47, as said below
- down_index: int32 [96, 12], P('tensor'), may hold values from 0 to 47, as said below
Outputs:
- input_grad: bfloat16 [6144, 6144], P(('dp', 'tensor'))
- grad_gate: float32 [96, 1536, 128], P('tensor', 'dp')
- grad_up: float32 [96, 1536, 128], P('tensor', 'dp')
- grad_down: float32 [96, 1536, 128], P('tensor', 'dp')
Inputs may be any that keep to these rules, and one draw needn't show every extreme that they name: `gate_index`: each row holds 12 different block numbers. `up_index`: each row holds 12 different block numbers. `down_index`: each row holds 12 different block numbers.
All inputs are finite; a program needn't handle non-finite values.
Results may differ from a plain program's by a relative error of at most 0.02.
Values may be sent and summed in bfloat16 or wider, within the bound.
No kernel may reach another device: no remote copies, remote signals or barrier semaphores. Data moves between devices by JAX's collectives and lax.ppermute only.
A program may use at most 256 MiB of HBM per device.

v0:
```python
import functools
import math

import jax
import jax.numpy as jnp
from jax import lax
from jax.experimental import pallas as pl
from jax.experimental.pallas import tpu as pltpu
from jax.sharding import PartitionSpec as P

BLK = 128
ROWS = 96
SET = 3 * ROWS
NNZ = 12
BF = jnp.bfloat16
F32 = jnp.float32
CHUNKS = (7,5)
VMEM_BYTES = 53 << 20
FULL_BYTES = 63 << 20
LONG = 200 * 10**9


def dot(a, b):
    return jnp.dot(a, b, preferred_element_type=F32)


def dot_nt(a, b):
    return lax.dot_general(a, b, (((1,), (1,)), ((), ())), preferred_element_type=F32)


def dot_tn(a, b):
    return lax.dot_general(a, b, (((0,), (0,)), ((), ())), preferred_element_type=F32)


def block_at(ref, block):
    return ref[:, pl.ds(pl.multiple_of(block * BLK, BLK), BLK)]


def chunk_kernel(
    first, scale,
    gate_ids, up_ids, down_ids, place,
    tok, out_grad, w_gate, w_up, w_down, *rest,
):
    far_p, far_m, plus, minus, own, gate_out, up_out, terms = rest[-8:]
    step = pl.program_id(0)
    j = first + step
    y, z, flip = place[0], place[1], place[2]

    def forward(source, ids, weight, transposed):
        half = source.shape[0] // 2
        return jnp.concatenate(
            [forward_rows(source, ids, weight, transposed, r, half) for r in (0, half)], axis=0
        )

    def forward_rows(source, ids, weight, transposed, row, rows):
        total = None
        for k in range(0, NNZ, 2):
            left = jnp.concatenate(
                [block_at(source, ids[j, k + i])[row : row + rows] for i in range(2)], axis=1
            )
            if transposed:
                right = jnp.concatenate([weight[0, k], weight[0, k + 1]], axis=1)
                part = dot_nt(left, right)
            else:
                part = dot(left, weight[0, k : k + 2].reshape(2 * BLK, BLK))
            total = part if total is None else total + part
        return total

    gate_lin = forward(tok, gate_ids, w_gate, False)
    up_lin = forward(tok, up_ids, w_up, False)

    hidden_grad = forward(out_grad, down_ids, w_down, True)
    sigmoid = jax.nn.sigmoid(gate_lin)
    activated = gate_lin * sigmoid
    hidden = (activated * up_lin).astype(BF)
    up_grad = (hidden_grad * activated).astype(BF)
    gate_grad = (
        hidden_grad * up_lin * sigmoid * (1.0 + gate_lin * (1.0 - sigmoid))
    ).astype(BF)
    gate_out[...] = gate_grad
    up_out[...] = up_grad
    hidden_t = hidden.T

    def put(z_rel, w, term):
        for shard in range(4):
            y_rel = lax.rem(shard - y + 4, 4)
            at = jnp.where(flip == 0, y_rel * 4 + z_rel, z_rel * 4 + y_rel)
            terms[at, w * ROWS : (w + 1) * ROWS] = term[shard * ROWS : (shard + 1) * ROWS]

    for z_rel in range(4):
        group = 3 * lax.rem(z + z_rel, 4)
        for w, (ids, grad) in enumerate(((gate_ids, gate_grad), (up_ids, up_grad))):
            left = jnp.concatenate([block_at(tok, ids[j, group + i]) for i in range(3)], axis=1)
            put(z_rel, w, (dot_tn(left, grad) * scale).astype(BF))
        right = jnp.concatenate(
            [block_at(out_grad, down_ids[j, group + i]) for i in range(3)], axis=1
        )
        wide = (dot(hidden_t, right) * scale).astype(BF)
        put(z_rel, 2, jnp.concatenate([wide[:, i * BLK : (i + 1) * BLK] for i in range(3)], axis=0))

    own[...] = terms[0:4]
    plus[...] = terms[4:8]
    far_p[...] = terms[8:10]
    far_m[...] = terms[10:12]
    minus[...] = terms[12:16]


def run_chunk(first, size, scale, ids, place, tok, out_grad, weights, grads, after):
    tokens = tok.shape[0]
    hbm = pl.BlockSpec(memory_space=pl.ANY)
    vmem = pl.BlockSpec(memory_space=pltpu.VMEM)
    weight = pl.BlockSpec((1, NNZ, BLK, BLK), lambda i, *_: (first + i, 0, 0, 0))
    hidden = pl.BlockSpec((tokens, BLK), lambda i, *_: (0, first + i))
    extra = [*(grads or ()), *after]

    def terms_of(n):
        return pl.BlockSpec((n, SET, BLK), lambda i, *_: (0, i, 0)), jax.ShapeDtypeStruct(
            (n, size * SET, BLK), BF
        )

    far, direct = terms_of(2), terms_of(4)
    grad_shape = jax.ShapeDtypeStruct((tokens, weights[0].shape[0] * BLK), BF)
    return pl.pallas_call(
        functools.partial(chunk_kernel, first, scale),
        grid_spec=pltpu.PrefetchScalarGridSpec(
            num_scalar_prefetch=4,
            grid=(size,),
            in_specs=[vmem] * 2 + [weight] * 3 + [hbm] * len(extra),
            out_specs=[far[0]] * 2 + [direct[0]] * 3 + [hidden] * 2,
            scratch_shapes=[pltpu.VMEM((16, SET, BLK), BF)],
        ),
        out_shape=[far[1]] * 2 + [direct[1]] * 3 + [grad_shape] * 2,
        input_output_aliases={9: 5, 10: 6} if grads else {},
        compiler_params=pltpu.CompilerParams(vmem_limit_bytes=VMEM_BYTES),
        cost_estimate=pl.CostEstimate(
            flops=size * NNZ * 12 * tokens * BLK * BLK, bytes_accessed=20 << 20, transcendentals=0
        ),
        name="chunk",
    )(*ids, place, tok, out_grad, *weights, *extra)


def back_kernel(gate_ids, up_ids, gate_grad, up_grad, w_gate, w_up, out, token, total, piece, sem):
    j = pl.program_id(0)
    rows, width = total.shape

    @pl.when(j == 0)
    def _():
        total[...] = jnp.zeros_like(total)
        token[...] = jnp.zeros_like(token)

    for ids, grad, weight in ((gate_ids, gate_grad, w_gate), (up_ids, up_grad, w_up)):
        for k in range(0, NNZ, 2):
            right = weight[0, k : k + 2].reshape(2 * BLK, BLK)
            part = jnp.concatenate(
                [dot_nt(grad[r : r + rows // 2], right) for r in (0, rows // 2)], axis=0
            )
            for i in range(2):
                at = pl.ds(pl.multiple_of(ids[j, k + i] * BLK, BLK), BLK)
                total[:, at] = total[:, at] + part[:, i * BLK : (i + 1) * BLK]

    @pl.when(j == pl.num_programs(0) - 1)
    def _():
        count = 4
        step = width // count
        copies = []
        for q in range(count):
            at = pl.ds(q * step, step)
            piece[q] = total[:, at].astype(BF)
            copies.append(pltpu.make_async_copy(piece.at[q], out.at[:, at], sem.at[q]))
            copies[-1].start()
        for copy in copies:
            copy.wait()


def run_back(ids, gate_grad, up_grad, w_gate, w_up, width, after):
    tokens = gate_grad.shape[0]
    blocks = w_gate.shape[0]
    hidden = pl.BlockSpec((tokens, BLK), lambda i, *_: (0, i))
    weight = pl.BlockSpec((1, NNZ, BLK, BLK), lambda i, *_: (i, 0, 0, 0))
    hbm = pl.BlockSpec(memory_space=pl.ANY)

    def kernel(*refs):
        back_kernel(*refs[:6], *refs[6 + len(after) :])

    return pl.pallas_call(
        kernel,
        grid_spec=pltpu.PrefetchScalarGridSpec(
            num_scalar_prefetch=2,
            grid=(blocks,),
            in_specs=[hidden, hidden, weight, weight] + [hbm] * len(after),
            out_specs=[hbm, pl.BlockSpec((8, BLK), lambda i, *_: (0, 0))],
            scratch_shapes=[
                pltpu.VMEM((tokens, width), F32),
                pltpu.VMEM((4, tokens, width // 4), BF),
                pltpu.SemaphoreType.DMA((4,)),
            ],
        ),
        out_shape=[
            jax.ShapeDtypeStruct((tokens, width), BF),
            jax.ShapeDtypeStruct((8, BLK), F32),
        ],
        compiler_params=pltpu.CompilerParams(vmem_limit_bytes=FULL_BYTES),
        cost_estimate=pl.CostEstimate(
            flops=blocks * NNZ * 4 * tokens * BLK * BLK, bytes_accessed=16 << 20, transcendentals=0
        ),
        name="back",
    )(*ids, gate_grad, up_grad, w_gate, w_up, *after)


def wide(a):
    return a[...].astype(F32)


def call(kernel, name, grid, in_specs, out_specs, out_shape, args, aliases=None, after=(), room=False, flops=0):
    taken = len(args)

    def run(*refs):
        kernel(*refs[:taken], *refs[taken + len(after) :])

    return pl.pallas_call(
        run,
        grid=grid,
        in_specs=in_specs + [pl.BlockSpec(memory_space=pl.ANY)] * len(after),
        out_specs=out_specs,
        out_shape=out_shape,
        input_output_aliases=aliases or {},
        compiler_params=pltpu.CompilerParams(vmem_limit_bytes=VMEM_BYTES if room else FULL_BYTES),
        cost_estimate=pl.CostEstimate(flops=flops, bytes_accessed=0, transcendentals=0),
        name=name,
    )(*args, *after)


def far_kernel(far_p, far_m, plus, minus, plus_out, minus_out):
    plus_out[...] = (wide(plus) + wide(far_p)).astype(BF)
    minus_out[...] = (wide(minus) + wide(far_m)).astype(BF)


def add_far(far_p, far_m, plus, minus, **order):
    rows = plus.shape[1]
    one = (1, rows, BLK)
    low = pl.BlockSpec(one, lambda i: (i, 0, 0))
    high = pl.BlockSpec(one, lambda i: (i + 2, 0, 0))
    shape = jax.ShapeDtypeStruct(plus.shape, BF)
    return call(
        far_kernel, "add_far", (2,), [low, low, low, high], [low, high], [shape, shape],
        (far_p, far_m, plus, minus), {2: 0, 3: 1}, **order,
    )


def near_kernel(own, got_p, got_m, far_p, far_m, plus, minus, kept):
    total = (wide(own) + wide(got_p) + wide(got_m)).astype(BF)
    kept[...] = total[0]
    plus[...] = total[1]
    minus[...] = total[3]

    @pl.when(pl.program_id(0) == 0)
    def _():
        far_p[...] = total[2]

    @pl.when(pl.program_id(0) == 1)
    def _():
        far_m[...] = total[2]


def add_near(own, got_p, got_m, **order):
    half = own.shape[1] // 2
    block = pl.BlockSpec((4, half, BLK), lambda i: (0, i, 0))
    part = pl.BlockSpec((half, BLK), lambda i: (i, 0))
    fixed = pl.BlockSpec((half, BLK), lambda i: (0, 0))
    small = jax.ShapeDtypeStruct((half, BLK), BF)
    large = jax.ShapeDtypeStruct((2 * half, BLK), BF)
    return call(
        near_kernel, "add_near", (2,), [block] * 3, [fixed] * 2 + [part] * 3,
        [small] * 2 + [large] * 3, (own, got_p, got_m), **order,
    )


def add_far2(far_p, far_m, plus, minus, **order):
    half = far_p.shape[0]
    whole = pl.BlockSpec((half, BLK), lambda i: (0, 0))
    high = pl.BlockSpec((half, BLK), lambda i: (1, 0))
    shape = jax.ShapeDtypeStruct(plus.shape, BF)
    return call(
        far_kernel, "add_far2", (1,), [whole, whole, whole, high], [whole, high], [shape, shape],
        (far_p, far_m, plus, minus), {2: 0, 3: 1}, **order,
    )


def last_kernel(size, kept, got_p, got_m, *outs):
    total = wide(kept) + wide(got_p) + wide(got_m)
    for i in range(size):
        for w in range(3):
            outs[w - 3][i] = total[i * SET + w * ROWS : i * SET + (w + 1) * ROWS]


def add_last(first, size, blocks, kept, got_p, got_m, grads, flops=0):
    whole = pl.BlockSpec(kept.shape, lambda i: (0, 0))
    step = math.gcd(first, size) if first else size
    hbm = pl.BlockSpec(memory_space=pl.ANY)
    spec = pl.BlockSpec((step, ROWS, BLK), lambda i: (first // step + i, 0, 0))
    part = pl.BlockSpec((step * SET, BLK), lambda i: (i, 0))
    shape = jax.ShapeDtypeStruct((blocks, ROWS, BLK), F32)
    given = [] if grads is None else list(grads)
    return call(
        functools.partial(last_kernel, step), "add_last", (size // step,),
        [part] * 3 + [hbm] * len(given), [spec] * 3, [shape] * 3,
        (kept, got_p, got_m, *given), {3 + i: i for i in range(len(given))}, flops=flops,
    )


def body(tokens, grad_out, gate_weight, up_weight, down_weight, gate_index, up_index, down_index):
    row_count, width = tokens.shape
    scale = 1.0 / math.sqrt(row_count * lax.axis_size("dp"))
    me, flip = lax.axis_index("dp"), lax.rem(lax.axis_index("tensor"), 2)
    place = jnp.stack([lax.rem(me, 4), lax.div(me, 4), flip]).astype(jnp.int32)
    ids = (gate_index, up_index, down_index)
    weights = (gate_weight, up_weight, down_weight)
    blocks = gate_weight.shape[0]

    def pairs(second, by):
        found = []
        for z in range(4):
            for y in range(4):
                for t in range(8):
                    along_y = (t % 2 == 0) != second
                    to = (z, (y + by) % 4) if along_y else ((z + by) % 4, y)
                    found.append(((z * 4 + y) * 8 + t, (to[0] * 4 + to[1]) * 8 + t))
        return found

    def send(up, down, second):
        axes = ("dp", "tensor")
        return (
            lax.ppermute(up, axes, pairs(second, 1)),
            lax.ppermute(down, axes, pairs(second, -1)),
        )

    starts = [sum(CHUNKS[:c]) for c in range(len(CHUNKS))]
    made, sent, grads = [], {}, None

    def chunk(c, *after):
        made.append(
            run_chunk(
                starts[c], CHUNKS[c], scale, ids, place, tokens, grad_out, weights,
                made[-1][5:] if made else None, after,
            )
        )

    def far(c, **order):
        far_p, far_m, plus, minus = made[c][:4]
        sent[c] = add_far(*send(far_p, far_m, False), plus, minus, **order)

    def near(c, **order):
        sent[c] = add_near(made[c][4], *send(*sent[c], False), **order)

    def far2(c, **order):
        far_p, far_m, plus, minus, kept = sent[c]
        sent[c] = (*add_far2(*send(far_p, far_m, True), plus, minus, **order), kept)

    def last(c, grads, flops=0):
        plus, minus, kept = sent[c]
        return add_last(starts[c], CHUNKS[c], blocks, kept, *send(plus, minus, True), grads, flops)

    chunk(0)
    chunk(1)
    far(0, after=(made[1][0],))
    partial, token = run_back(
        ids[:2], *made[1][5:], gate_weight, up_weight, width, (sent[0][0],)
    )
    summed = lax.psum_scatter(partial, "tensor", scatter_dimension=0, tiled=True)
    far(1, after=(token,), flops=LONG)
    near(0, after=(sent[1][0],))
    far2(0)
    near(1, after=(sent[0][0],))
    grads = last(0, grads)
    far2(1)
    grads = last(1, grads)
    return (summed, *grads)


def solution(mesh):
    in_specs = (
        P("dp", None),
        P("dp", None),
        P("tensor", None, None, None),
        P("tensor", None, None, None),
        P("tensor", None, None, None),
        P("tensor", None),
        P("tensor", None),
        P("tensor", None),
    )
    out_specs = (
        P(("dp", "tensor"), None),
        P("tensor", "dp", None),
        P("tensor", "dp", None),
        P("tensor", "dp", None),
    )
    return jax.shard_map(body, mesh=mesh, in_specs=in_specs, out_specs=out_specs, check_vma=False)
```

profile of v0, /device:TPU:0, one launch (start us, length us, event | category | flops | bytes accessed | tf_op | source)
XLA Modules:
  0.0 151.5 jit_solution(16520983301114194182)
XLA Ops:
  7.2 0.0 reduce-scatter.2.cloned.1.call-start
  7.2 0.1 pad_add_fusion.place
  7.3 0.7 copy-done.1
  8.0 0.7 copy-done.2
  8.7 0.7 copy-done.3
  9.4 25.5 %chunk.2 = (bf16[2,2016,128]{2,1,0:T(8,128)(2,1)}, bf16[2,2016,128]{2,1,0:T(8,128)(2,1)}, bf16[4,2016,128]{2,1,0:T(8,128)(2,1)}, bf16[4,2016,128]{2,1,0:T(8,128)...) custom-call(s32[12,12]{1,0:T(8,128)S(1)} %copy-done.1, ...), custom_call_target="tpu_custom_call" | custom-call | flops 6341787648 | bytes 20971520 | tf_op jit(solution)/shard_map/chunk/pallas_call | solution.py:123
  34.9 1.7 %collective-permute-start = (bf16[2,2016,128]{2,1,0:T(8,128)(2,1)}, bf16[2,2016,128]{2,1,0:T(8,128)(2,1)}, u32[]{:S(2)}, u32[]{:S(2)}) collective-permute-start(bf16[2,2016,128]{2,1,0:T(8,128)(2,1)} %get-tuple-element.48), channel_id=1, source_target_pairs={{0,8},{1,33},{2,10},{3,35},{4,12},{5,37},{6,14},{7,39},{8,16},{9,4... | collective-permute-start | bytes 3096584 | tf_op jit(solution)/shard_map/ppermute | solution.py:333
  36.6 1.6 %collective-permute-start.1 = (bf16[2,2016,128]{2,1,0:T(8,128)(2,1)}, bf16[2,2016,128]{2,1,0:T(8,128)(2,1)}, u32[]{:S(2)}, u32[]{:S(2)}) collective-permute-start(bf16[2,2016,128]{2,1,0:T(8,128)(2,1)} %get-tuple-element.49), channel_id=1, source_target_pairs={{0,24},{1,97},{2,26},{3,99},{4,28},{5,101},{6,30},{7,103},{8,0},{9... | collective-permute-start | bytes 3096584 | tf_op jit(solution)/shard_map/ppermute | solution.py:334
  38.2 20.1 %chunk.3 = (bf16[2,1440,128]{2,1,0:T(8,128)(2,1)S(1)}, bf16[2,1440,128]{2,1,0:T(8,128)(2,1)}, bf16[4,1440,128]{2,1,0:T(8,128)(2,1)}, bf16[4,1440,128]{2,1,0:T(8,...) custom-call(s32[12,12]{1,0:T(8,128)S(1)} %copy-done.1, ...), custom_call_target="tpu_custom_call", output_to_operand_aliasing={{5}: (9, {}), {6}: (10, {})} | custom-call | flops 4529848320 | bytes 20971520 | tf_op jit(solution)/shard_map/chunk/pallas_call | solution.py:123
  58.2 0.5 collective-permute-start.2
  58.7 2.8 %collective-permute-start.3 = (bf16[2,1440,128]{2,1,0:T(8,128)(2,1)}, bf16[2,1440,128]{2,1,0:T(8,128)(2,1)}, u32[]{:S(2)}, u32[]{:S(2)}) collective-permute-start(bf16[2,1440,128]{2,1,0:T(8,128)(2,1)} %get-tuple-element.56), channel_id=1, source_target_pairs={{0,24},{1,97},{2,26},{3,99},{4,28},{5,101},{6,30},{7,103},{8,0},{9... | collective-permute-start | bytes 2211848 | tf_op jit(solution)/shard_map/ppermute | solution.py:334
  61.5 0.0 collective-permute-done.refs_0_
  61.5 0.0 collective-permute-done.1.refs_1_
  61.5 3.3 %add_far.2 = (bf16[4,2016,128]{2,1,0:T(8,128)(2,1)}, bf16[4,2016,128]{2,1,0:T(8,128)(2,1)}) custom-call(bf16[2,2016,128]{2,1,0:T(8,128)(2,1)} %collective-permute-done.refs_0_, bf16[2,2016,128]{2,1,0:T(8,128)(2,1)} %collective-permute-done.1.refs_1_, bf16[4,2016,128]{2,1,0:T(8,128)(2,1)} %get-tuple-element.50.refs_2_, ...), custom_call_target="tpu_custom_call", output_to_operand_aliasing={{0}: (2, {}), {1}: (3, {})} | custom-call | tf_op jit(solution)/shard_map/add_far/pallas_call | solution.py:220
  64.9 3.2 %collective-permute-start.7 = (bf16[4,2016,128]{2,1,0:T(8,128)(2,1)}, bf16[4,2016,128]{2,1,0:T(8,128)(2,1)}, u32[]{:S(2)}, u32[]{:S(2)}) collective-permute-start(bf16[4,2016,128]{2,1,0:T(8,128)(2,1)} %get-tuple-element.63), channel_id=1, source_target_pairs={{0,24},{1,97},{2,26},{3,99},{4,28},{5,101},{6,30},{7,103},{8,0},{9... | collective-permute-start | bytes 6193160 | tf_op jit(solution)/shard_map/ppermute | solution.py:334
  68.1 22.5 %back.1 = (bf16[384,6144]{1,0:T(8,128)(2,1)}, f32[8,128]{1,0:T(8,128)}) custom-call(s32[12,12]{1,0:T(8,128)} %refs_0_.1, s32[12,12]{1,0:T(8,128)} %refs_1_.1, bf16[384,1536]{1,0:T(8,128)(2,1)} %get-tuple-element.46.refs_2_, bf16[384,1536]{1,0:T(8,128)(2,1)} %get-tuple-element.47.refs_3_, bf16[12,12,128,128]{3,2,1,0:T(8,128)(2,1)} %refs_4_.1, ...), custom_call_target="tpu_custom_call" | custom-call | flops 3623878656 | bytes 16777216 | tf_op jit(solution)/shard_map/back/pallas_call | solution.py:185
  90.6 0.0 reduce-scatter.2.cloned.1.call-update
  90.6 0.0 collective-permute-done.2.refs_0_
  90.6 0.0 collective-permute-done.3.refs_1_
  90.6 2.8 %add_far.3 = (bf16[4,1440,128]{2,1,0:T(8,128)(2,1)}, bf16[4,1440,128]{2,1,0:T(8,128)(2,1)}) custom-call(bf16[2,1440,128]{2,1,0:T(8,128)(2,1)} %collective-permute-done.2.refs_0_, bf16[2,1440,128]{2,1,0:T(8,128)(2,1)} %collective-permute-done.3.refs_1_, ...), custom_call_target="tpu_custom_call", output_to_operand_aliasing={{0}: (2, {}), {1}: (3, {})} | custom-call | flops 199999995904 | tf_op jit(solution)/shard_map/add_far/pallas_call | solution.py:220
  93.4 0.0 collective-permute-start.4
  93.4 3.2 %collective-permute-start.5 = (bf16[4,1440,128]{2,1,0:T(8,128)(2,1)}, bf16[4,1440,128]{2,1,0:T(8,128)(2,1)}, u32[]{:S(2)}, u32[]{:S(2)}) collective-permute-start(bf16[4,1440,128]{2,1,0:T(8,128)(2,1)} %get-tuple-element.61), channel_id=1, source_target_pairs={{0,24},{1,97},{2,26},{3,99},{4,28},{5,101},{6,30},{7,103},{8,0},{9... | collective-permute-start | bytes 4423688 | tf_op jit(solution)/shard_map/ppermute | solution.py:334
  96.6 4.4 %add_near.2 = (bf16[1008,128]{1,0:T(8,128)(2,1)}, bf16[1008,128]{1,0:T(8,128)(2,1)}, bf16[2016,128]{1,0:T(8,128)(2,1)}, bf16[2016,128]{1,0:T(8,128)(2,1)}, bf16[2016,128]{1,0:T(8,128)(2,1)}) custom-call(bf16[4,2016,128]{2,1,0:T(8,128)(2,1)} %get-tuple-element.62.refs_0_, bf16[4,2016,128]{2,1,0:T(8,128)(2,1)} %collective-permute-done.6.refs_1_, ...), custom_call_target="tpu_custom_call" | custom-call | tf_op jit(solution)/shard_map/add_near/pallas_call | solution.py:220
  101.0 2.3 %collective-permute-start.8 = (bf16[1008,128]{1,0:T(8,128)(2,1)}, bf16[1008,128]{1,0:T(8,128)(2,1)S(1)}, u32[]{:S(2)}, u32[]{:S(2)}) collective-permute-start(bf16[1008,128]{1,0:T(8,128)(2,1)} %get-tuple-element.64), channel_id=1, source_target_pairs={{0,32},{1,9},{2,34},{3,11},{4,36},{5,13},{6,38},{7,15},{8,40},{9,1... | collective-permute-start | bytes 774152 | tf_op jit(solution)/shard_map/ppermute | solution.py:333
  103.3 2.3 %collective-permute-start.9 = (bf16[1008,128]{1,0:T(8,128)(2,1)}, bf16[1008,128]{1,0:T(8,128)(2,1)S(1)}, u32[]{:S(2)}, u32[]{:S(2)}) collective-permute-start(bf16[1008,128]{1,0:T(8,128)(2,1)} %get-tuple-element.65), channel_id=1, source_target_pairs={{0,96},{1,25},{2,98},{3,27},{4,100},{5,29},{6,102},{7,31},{8,104},... | collective-permute-start | bytes 774152 | tf_op jit(solution)/shard_map/ppermute | solution.py:334
  105.5 7.3 %collective-permute-done.8.refs_0_ = bf16[1008,128]{1,0:T(8,128)(2,1)S(1)} collective-permute-done((bf16[1008,128]{1,0:T(8,128)(2,1)}, bf16[1008,128]{1,0:T(8,128)(2,1)S(1)}, u32[]{:S(2)}, u32[]{:S(2)}) %collective-permute-start.8) | collective-permute-done | bytes 258080 | tf_op jit(solution)/shard_map/ppermute | solution.py:333
  112.8 0.0 collective-permute-done.9.refs_1_
  112.8 0.7 copy-done.6
  113.5 0.1 copy-done.7
  113.6 2.2 %add_far2.2 = (bf16[2016,128]{1,0:T(8,128)(2,1)}, bf16[2016,128]{1,0:T(8,128)(2,1)}) custom-call(bf16[1008,128]{1,0:T(8,128)(2,1)} %copy-done.6, bf16[1008,128]{1,0:T(8,128)(2,1)} %copy-done.7, bf16[2016,128]{1,0:T(8,128)(2,1)} %get-tuple-element.66.refs_2_, bf16[2016,128]{1,0:T(8,128)(2,1)} %get-tuple-element.67.refs_3_), custom_call_target="tpu_custom_call", output_to_operand_aliasing={{0}: (2, {}), {1}: (3, {})} | custom-call | tf_op jit(solution)/shard_map/add_far2/pallas_call | solution.py:220
  115.8 1.2 collective-permute-done.4.refs_1_
  117.0 0.0 collective-permute-done.5.refs_2_
  117.1 3.6 %add_near.3 = (bf16[720,128]{1,0:T(8,128)(2,1)}, bf16[720,128]{1,0:T(8,128)(2,1)}, bf16[1440,128]{1,0:T(8,128)(2,1)}, bf16[1440,128]{1,0:T(8,128)(2,1)}, bf16[1440,128]{1,0:T(8,128)(2,1)}) custom-call(bf16[4,1440,128]{2,1,0:T(8,128)(2,1)} %get-tuple-element.55.refs_0_, bf16[4,1440,128]{2,1,0:T(8,128)(2,1)} %collective-permute-done.4.refs_1_, ...), custom_call_target="tpu_custom_call" | custom-call | tf_op jit(solution)/shard_map/add_near/pallas_call | solution.py:220
  120.6 1.9 %collective-permute-start.10 = (bf16[720,128]{1,0:T(8,128)(2,1)}, bf16[720,128]{1,0:T(8,128)(2,1)S(1)}, u32[]{:S(2)}, u32[]{:S(2)}) collective-permute-start(bf16[720,128]{1,0:T(8,128)(2,1)} %get-tuple-element.70), channel_id=1, source_target_pairs={{0,32},{1,9},{2,34},{3,11},{4,36},{5,13},{6,38},{7,15},{8,40},{9,1... | collective-permute-start | bytes 552968 | tf_op jit(solution)/shard_map/ppermute | solution.py:333
  122.6 2.1 %collective-permute-start.11 = (bf16[720,128]{1,0:T(8,128)(2,1)}, bf16[720,128]{1,0:T(8,128)(2,1)S(1)}, u32[]{:S(2)}, u32[]{:S(2)}) collective-permute-start(bf16[720,128]{1,0:T(8,128)(2,1)} %get-tuple-element.71), channel_id=1, source_target_pairs={{0,96},{1,25},{2,98},{3,27},{4,100},{5,29},{6,102},{7,31},{8,104},... | collective-permute-start | bytes 552968 | tf_op jit(solution)/shard_map/ppermute | solution.py:334
  124.7 3.2 %collective-permute-start.15 = (bf16[2016,128]{1,0:T(8,128)(2,1)}, bf16[2016,128]{1,0:T(8,128)(2,1)}, u32[]{:S(2)}, u32[]{:S(2)}) collective-permute-start(bf16[2016,128]{1,0:T(8,128)(2,1)} %get-tuple-element.77), channel_id=1, source_target_pairs={{0,96},{1,25},{2,98},{3,27},{4,100},{5,29},{6,102},{7,31},{8,104},... | collective-permute-start | bytes 1548296 | tf_op jit(solution)/shard_map/ppermute | solution.py:334
  127.9 0.4 collective-permute-done.10.refs_0_
  128.4 0.7 copy-done.8
  129.0 0.1 copy-done.9
  129.1 2.0 %add_far2.3 = (bf16[1440,128]{1,0:T(8,128)(2,1)}, bf16[1440,128]{1,0:T(8,128)(2,1)}) custom-call(bf16[720,128]{1,0:T(8,128)(2,1)} %copy-done.8, bf16[720,128]{1,0:T(8,128)(2,1)} %copy-done.9, bf16[1440,128]{1,0:T(8,128)(2,1)} %get-tuple-element.72.refs_2_, bf16[1440,128]{1,0:T(8,128)(2,1)} %get-tuple-element.73.refs_3_), custom_call_target="tpu_custom_call", output_to_operand_aliasing={{0}: (2, {}), {1}: (3, {})} | custom-call | tf_op jit(solution)/shard_map/add_far2/pallas_call | solution.py:220
  131.1 1.8 %collective-permute-start.12 = (bf16[1440,128]{1,0:T(8,128)(2,1)}, bf16[1440,128]{1,0:T(8,128)(2,1)S(1)}, u32[]{:S(2)}, u32[]{:S(2)}) collective-permute-start(bf16[1440,128]{1,0:T(8,128)(2,1)} %get-tuple-element.74), channel_id=1, source_target_pairs={{0,32},{1,9},{2,34},{3,11},{4,36},{5,13},{6,38},{7,15},{8,40},{9,1... | collective-permute-start | bytes 1105928 | tf_op jit(solution)/shard_map/ppermute | solution.py:333
  132.9 1.4 collective-permute-start.13
  134.4 0.8 collective-permute-done.14.refs_1_
  135.1 2.4 %add_last.2 = (f32[12,96,128]{2,1,0:T(8,128)}, f32[12,96,128]{2,1,0:T(8,128)}, f32[12,96,128]{2,1,0:T(8,128)}) custom-call(bf16[2016,128]{1,0:T(8,128)(2,1)} %get-tuple-element.76.refs_0_, bf16[2016,128]{1,0:T(8,128)(2,1)} %collective-permute-done.14.refs_1_, bf16[2016,128]{1,0:T(8,128)(2,1)} %collective-permute-done.15.refs_2_), custom_call_target="tpu_custom_call" | custom-call | tf_op jit(solution)/shard_map/add_last/pallas_call | solution.py:220
  137.5 2.6 %collective-permute-done.12.refs_1_ = bf16[1440,128]{1,0:T(8,128)(2,1)S(1)} collective-permute-done((bf16[1440,128]{1,0:T(8,128)(2,1)}, bf16[1440,128]{1,0:T(8,128)(2,1)S(1)}, u32[]{:S(2)}, u32[]{:S(2)}) %collective-permute-start.12) | collective-permute-done | bytes 368672 | tf_op jit(solution)/shard_map/ppermute | solution.py:333
  140.1 0.7 collective-permute-done.13.refs_2_
  140.8 0.1 copy-done.5
  140.8 3.8 %add_last.3 = (f32[12,96,128]{2,1,0:T(8,128)}, f32[12,96,128]{2,1,0:T(8,128)}, f32[12,96,128]{2,1,0:T(8,128)}) custom-call(bf16[1440,128]{1,0:T(8,128)(2,1)} %get-tuple-element.69.refs_0_, bf16[1440,128]{1,0:T(8,128)(2,1)} %copy-done.5, ...), custom_call_target="tpu_custom_call", output_to_operand_aliasing={{0}: (3, {}), {1}: (4, {}), {2}: (5, {})} | custom-call | tf_op jit(solution)/shard_map/add_last/pallas_call | solution.py:220
  (19 shorter events, 0.0 us)
Async XLA Ops:
  7.2 137.4 %reduce-scatter.2.cloned.1.call-start = ((), (), s32[]{:S(2)}) async-start(), calls=%async_computation.1 | async-start | bytes 5308416 | tf_op jit(solution)/shard_map/reduce_scatter | solution.py:369
  7.3 0.7 copy-start.1
  8.0 0.7 copy-start.2
  8.7 0.7 copy-start.3
  34.9 26.7 %collective-permute-start = (bf16[2,2016,128]{2,1,0:T(8,128)(2,1)}, bf16[2,2016,128]{2,1,0:T(8,128)(2,1)}, u32[]{:S(2)}, u32[]{:S(2)}) collective-permute-start(bf16[2,2016,128]{2,1,0:T(8,128)(2,1)} %get-tuple-element.48), channel_id=1, source_target_pairs={{0,8},{1,33},{2,10},{3,35},{4,12},{5,37},{6,14},{7,39},{8,16},{9,4... | collective-permute-start | bytes 3096584 | tf_op jit(solution)/shard_map/ppermute | solution.py:333
  36.6 25.0 %collective-permute-start.1 = (bf16[2,2016,128]{2,1,0:T(8,128)(2,1)}, bf16[2,2016,128]{2,1,0:T(8,128)(2,1)}, u32[]{:S(2)}, u32[]{:S(2)}) collective-permute-start(bf16[2,2016,128]{2,1,0:T(8,128)(2,1)} %get-tuple-element.49), channel_id=1, source_target_pairs={{0,24},{1,97},{2,26},{3,99},{4,28},{5,101},{6,30},{7,103},{8,0},{9... | collective-permute-start | bytes 3096584 | tf_op jit(solution)/shard_map/ppermute | solution.py:334
  58.2 3.3 %copy-start = (bf16[2,1440,128]{2,1,0:T(8,128)(2,1)}, bf16[2,1440,128]{2,1,0:T(8,128)(2,1)S(1)}, u32[]{:S(2)}) copy-start(bf16[2,1440,128]{2,1,0:T(8,128)(2,1)S(1)} %get-tuple-element.52.refs_4_) | copy-start | bytes 2211844
  58.2 32.4 %collective-permute-start.2 = (bf16[2,1440,128]{2,1,0:T(8,128)(2,1)S(1)}, bf16[2,1440,128]{2,1,0:T(8,128)(2,1)}, u32[]{:S(2)}, u32[]{:S(2)}) collective-permute-start(bf16[2,1440,128]{2,1,0:T(8,128)(2,1)S(1)} %get-tuple-element.52.refs_4_), channel_id=1, source_target_pairs={{0,8},{1,33},{2,10},{3,35},{4,12},{5,37},{6,14},{7,39},{8,16},{9,4... | collective-permute-start | bytes 2211848 | tf_op jit(solution)/shard_map/ppermute | solution.py:333
  58.7 31.9 %collective-permute-start.3 = (bf16[2,1440,128]{2,1,0:T(8,128)(2,1)}, bf16[2,1440,128]{2,1,0:T(8,128)(2,1)}, u32[]{:S(2)}, u32[]{:S(2)}) collective-permute-start(bf16[2,1440,128]{2,1,0:T(8,128)(2,1)} %get-tuple-element.56), channel_id=1, source_target_pairs={{0,24},{1,97},{2,26},{3,99},{4,28},{5,101},{6,30},{7,103},{8,0},{9... | collective-permute-start | bytes 2211848 | tf_op jit(solution)/shard_map/ppermute | solution.py:334
  64.8 31.8 %collective-permute-start.6 = (bf16[4,2016,128]{2,1,0:T(8,128)(2,1)}, bf16[4,2016,128]{2,1,0:T(8,128)(2,1)}, u32[]{:S(2)}, u32[]{:S(2)}) collective-permute-start(bf16[4,2016,128]{2,1,0:T(8,128)(2,1)} %get-tuple-element.53.refs_6_), channel_id=1, source_target_pairs={{0,8},{1,33},{2,10},{3,35},{4,12},{5,37},{6,14},{7,39},{8,16},{9,4... | collective-permute-start | bytes 6193160 | tf_op jit(solution)/shard_map/ppermute | solution.py:333
  64.9 31.8 %collective-permute-start.7 = (bf16[4,2016,128]{2,1,0:T(8,128)(2,1)}, bf16[4,2016,128]{2,1,0:T(8,128)(2,1)}, u32[]{:S(2)}, u32[]{:S(2)}) collective-permute-start(bf16[4,2016,128]{2,1,0:T(8,128)(2,1)} %get-tuple-element.63), channel_id=1, source_target_pairs={{0,24},{1,97},{2,26},{3,99},{4,28},{5,101},{6,30},{7,103},{8,0},{9... | collective-permute-start | bytes 6193160 | tf_op jit(solution)/shard_map/ppermute | solution.py:334
  93.4 23.7 %collective-permute-start.4 = (bf16[4,1440,128]{2,1,0:T(8,128)(2,1)}, bf16[4,1440,128]{2,1,0:T(8,128)(2,1)}, u32[]{:S(2)}, u32[]{:S(2)}) collective-permute-start(bf16[4,1440,128]{2,1,0:T(8,128)(2,1)} %get-tuple-element.60.refs_3_), channel_id=1, source_target_pairs={{0,8},{1,33},{2,10},{3,35},{4,12},{5,37},{6,14},{7,39},{8,16},{9,4... | collective-permute-start | bytes 4423688 | tf_op jit(solution)/shard_map/ppermute | solution.py:333
  93.4 23.7 %collective-permute-start.5 = (bf16[4,1440,128]{2,1,0:T(8,128)(2,1)}, bf16[4,1440,128]{2,1,0:T(8,128)(2,1)}, u32[]{:S(2)}, u32[]{:S(2)}) collective-permute-start(bf16[4,1440,128]{2,1,0:T(8,128)(2,1)} %get-tuple-element.61), channel_id=1, source_target_pairs={{0,24},{1,97},{2,26},{3,99},{4,28},{5,101},{6,30},{7,103},{8,0},{9... | collective-permute-start | bytes 4423688 | tf_op jit(solution)/shard_map/ppermute | solution.py:334
  101.0 11.8 %collective-permute-start.8 = (bf16[1008,128]{1,0:T(8,128)(2,1)}, bf16[1008,128]{1,0:T(8,128)(2,1)S(1)}, u32[]{:S(2)}, u32[]{:S(2)}) collective-permute-start(bf16[1008,128]{1,0:T(8,128)(2,1)} %get-tuple-element.64), channel_id=1, source_target_pairs={{0,32},{1,9},{2,34},{3,11},{4,36},{5,13},{6,38},{7,15},{8,40},{9,1... | collective-permute-start | bytes 774152 | tf_op jit(solution)/shard_map/ppermute | solution.py:333
  103.3 9.5 %collective-permute-start.9 = (bf16[1008,128]{1,0:T(8,128)(2,1)}, bf16[1008,128]{1,0:T(8,128)(2,1)S(1)}, u32[]{:S(2)}, u32[]{:S(2)}) collective-permute-start(bf16[1008,128]{1,0:T(8,128)(2,1)} %get-tuple-element.65), channel_id=1, source_target_pairs={{0,96},{1,25},{2,98},{3,27},{4,100},{5,29},{6,102},{7,31},{8,104},... | collective-permute-start | bytes 774152 | tf_op jit(solution)/shard_map/ppermute | solution.py:334
  112.8 0.7 copy-start.6
  112.8 0.8 copy-start.7
  117.1 7.7 %copy-start.4 = (bf16[2016,128]{1,0:T(8,128)(2,1)S(1)}, bf16[2016,128]{1,0:T(8,128)(2,1)}, u32[]{:S(2)}) copy-start(bf16[2016,128]{1,0:T(8,128)(2,1)} %get-tuple-element.68.refs_3_) | copy-start | bytes 1548292
  120.6 7.7 %collective-permute-start.10 = (bf16[720,128]{1,0:T(8,128)(2,1)}, bf16[720,128]{1,0:T(8,128)(2,1)S(1)}, u32[]{:S(2)}, u32[]{:S(2)}) collective-permute-start(bf16[720,128]{1,0:T(8,128)(2,1)} %get-tuple-element.70), channel_id=1, source_target_pairs={{0,32},{1,9},{2,34},{3,11},{4,36},{5,13},{6,38},{7,15},{8,40},{9,1... | collective-permute-start | bytes 552968 | tf_op jit(solution)/shard_map/ppermute | solution.py:333
  122.6 5.8 %collective-permute-start.11 = (bf16[720,128]{1,0:T(8,128)(2,1)}, bf16[720,128]{1,0:T(8,128)(2,1)S(1)}, u32[]{:S(2)}, u32[]{:S(2)}) collective-permute-start(bf16[720,128]{1,0:T(8,128)(2,1)} %get-tuple-element.71), channel_id=1, source_target_pairs={{0,96},{1,25},{2,98},{3,27},{4,100},{5,29},{6,102},{7,31},{8,104},... | collective-permute-start | bytes 552968 | tf_op jit(solution)/shard_map/ppermute | solution.py:334
  124.7 10.4 %collective-permute-start.14 = (bf16[2016,128]{1,0:T(8,128)(2,1)S(1)}, bf16[2016,128]{1,0:T(8,128)(2,1)}, u32[]{:S(2)}, u32[]{:S(2)}) collective-permute-start(bf16[2016,128]{1,0:T(8,128)(2,1)S(1)} %copy-done.4), channel_id=1, source_target_pairs={{0,32},{1,9},{2,34},{3,11},{4,36},{5,13},{6,38},{7,15},{8,40},{9,1... | collective-permute-start | bytes 1548296 | tf_op jit(solution)/shard_map/ppermute | solution.py:333
  124.7 10.4 %collective-permute-start.15 = (bf16[2016,128]{1,0:T(8,128)(2,1)}, bf16[2016,128]{1,0:T(8,128)(2,1)}, u32[]{:S(2)}, u32[]{:S(2)}) collective-permute-start(bf16[2016,128]{1,0:T(8,128)(2,1)} %get-tuple-element.77), channel_id=1, source_target_pairs={{0,96},{1,25},{2,98},{3,27},{4,100},{5,29},{6,102},{7,31},{8,104},... | collective-permute-start | bytes 1548296 | tf_op jit(solution)/shard_map/ppermute | solution.py:334
  128.4 0.7 copy-start.8
  128.4 0.7 copy-start.9
  131.1 9.0 %collective-permute-start.12 = (bf16[1440,128]{1,0:T(8,128)(2,1)}, bf16[1440,128]{1,0:T(8,128)(2,1)S(1)}, u32[]{:S(2)}, u32[]{:S(2)}) collective-permute-start(bf16[1440,128]{1,0:T(8,128)(2,1)} %get-tuple-element.74), channel_id=1, source_target_pairs={{0,32},{1,9},{2,34},{3,11},{4,36},{5,13},{6,38},{7,15},{8,40},{9,1... | collective-permute-start | bytes 1105928 | tf_op jit(solution)/shard_map/ppermute | solution.py:333
  132.9 7.8 %collective-permute-start.13 = (bf16[1440,128]{1,0:T(8,128)(2,1)}, bf16[1440,128]{1,0:T(8,128)(2,1)}, u32[]{:S(2)}, u32[]{:S(2)}) collective-permute-start(bf16[1440,128]{1,0:T(8,128)(2,1)} %get-tuple-element.75), channel_id=1, source_target_pairs={{0,96},{1,25},{2,98},{3,27},{4,100},{5,29},{6,102},{7,31},{8,104},... | collective-permute-start | bytes 1105928 | tf_op jit(solution)/shard_map/ppermute | solution.py:334
  140.1 0.8 copy-start.5
Sparse Core Ops, SparseCore 0:
  90.7 39.3 reduce-scatter.1
where the time goes:
time: 152 us; the launch traced here: 151 us
  Pallas kernels  92.4 us (61%)
  starting transfers between devices  28.2 us (19%)
  between operations  14.1 us (9%)
  waiting for transfers between devices  13 us (9%)
  local copies, waits for them, and re-layouts  3.67 us (2%)
    pallas_call x2, Pallas kernels, run_chunk(): pl.pallas_call(functools.partial(chunk_kernel, first, scale), grid_spec=p...  45.6 us
    pallas_call x8, Pallas kernels, call(): pl.pallas_call(run, grid=grid, in_specs=in_specs + [pl.BlockSpec(memory_s...  24.4 us
    pallas_call x1, Pallas kernels, run_back(): pl.pallas_call(kernel, grid_spec=pltpu.PrefetchScalarGridSpec(num_scalar_...  22.5 us
    ppermute x8, starting transfers between devices, send(): lax.ppermute(down, axes, pairs(second, -1))  19.9 us
    ppermute x8, waiting for transfers between devices, send(): lax.ppermute(up, axes, pairs(second, 1))  12.3 us
    ppermute x8, starting transfers between devices, send(): lax.ppermute(up, axes, pairs(second, 1))  8.23 us
    unnamed x20, local copies, waits for them, and re-layouts  3.67 us
  transfers between devices with their start and end apart: 17, of which 6 were waited for; matrix products, arithmetic and copies ran while one was open for 0% of the time, Pallas kernels for 44%

commit v1 on v0

--- a/solution.py
+++ b/solution.py
@@ -16,7 +16,7 @@
 F32 = jnp.float32
 CHUNKS = (7,5)
 VMEM_BYTES = 53 << 20
-FULL_BYTES = 63 << 20
+FULL_BYTES = (64 << 20) - (64 << 10)
 LONG = 200 * 10**9
 
 
@@ -26,10 +26,6 @@
 
 def dot_nt(a, b):
     return lax.dot_general(a, b, (((1,), (1,)), ((), ())), preferred_element_type=F32)
-
-
-def dot_tn(a, b):
-    return lax.dot_general(a, b, (((0,), (0,)), ((), ())), preferred_element_type=F32)
 
 
 def block_at(ref, block):
@@ -79,7 +75,7 @@
     ).astype(BF)
     gate_out[...] = gate_grad
     up_out[...] = up_grad
-    hidden_t = hidden.T
+    hidden_t, gate_t, up_t = hidden.T, gate_grad.T, up_grad.T
 
     def put(z_rel, w, term):
         for shard in range(4):
@@ -89,14 +85,17 @@
 
     for z_rel in range(4):
         group = 3 * lax.rem(z + z_rel, 4)
-        for w, (ids, grad) in enumerate(((gate_ids, gate_grad), (up_ids, up_grad))):
-            left = jnp.concatenate([block_at(tok, ids[j, group + i]) for i in range(3)], axis=1)
-            put(z_rel, w, (dot_tn(left, grad) * scale).astype(BF))
-        right = jnp.concatenate(
-            [block_at(out_grad, down_ids[j, group + i]) for i in range(3)], axis=1
-        )
-        wide = (dot(hidden_t, right) * scale).astype(BF)
-        put(z_rel, 2, jnp.concatenate([wide[:, i * BLK : (i + 1) * BLK] for i in range(3)], axis=0))
+        wide = []
+        for left, source, ids in (
+            (gate_t, tok, gate_ids), (up_t, tok, up_ids), (hidden_t, out_grad, down_ids)
+        ):
+            right = jnp.concatenate(
+                [block_at(source, ids[j, group + i]) for i in range(3)], axis=1
+            )
+            wide.append((dot(left, right) * scale).astype(BF))
+        for w, term in enumerate(wide):
+            parts = [term[:, i * BLK : (i + 1) * BLK] for i in range(3)]
+            put(z_rel, w, jnp.concatenate(parts if w == 2 else [p.T for p in parts], axis=0))
 
     own[...] = terms[0:4]
     plus[...] = terms[4:8]
@@ -133,7 +132,7 @@
         input_output_aliases={9: 5, 10: 6} if grads else {},
         compiler_params=pltpu.CompilerParams(vmem_limit_bytes=VMEM_BYTES),
         cost_estimate=pl.CostEstimate(
-            flops=size * NNZ * 12 * tokens * BLK * BLK, bytes_accessed=20 << 20, transcendentals=0
+            flops=25 * 10**9, bytes_accessed=20 << 20, transcendentals=0
         ),
         name="chunk",
     )(*ids, place, tok, out_grad, *weights, *extra)
@@ -201,7 +200,7 @@
         ],
         compiler_params=pltpu.CompilerParams(vmem_limit_bytes=FULL_BYTES),
         cost_estimate=pl.CostEstimate(
-            flops=blocks * NNZ * 4 * tokens * BLK * BLK, bytes_accessed=16 << 20, transcendentals=0
+            flops=25 * 10**9, bytes_accessed=16 << 20, transcendentals=0
         ),
         name="back",
     )(*ids, gate_grad, up_grad, w_gate, w_up, *after)
@@ -286,52 +285,68 @@
     )
 
 
-def last_kernel(size, kept, got_p, got_m, *outs):
-    total = wide(kept) + wide(got_p) + wide(got_m)
-    for i in range(size):
-        for w in range(3):
-            outs[w - 3][i] = total[i * SET + w * ROWS : i * SET + (w + 1) * ROWS]
-
-
-def add_last(first, size, blocks, kept, got_p, got_m, grads, flops=0):
+def last_kernel(first, size, kept, got_p, got_m, *refs):
+    outs, total, sem = refs[-5:-2], refs[-2], refs[-1]
+    sums = wide(kept) + wide(got_p) + wide(got_m)
+    copies = []
+    for w in range(3):
+        for i in range(size):
+            total[w, i] = sums[i * SET + w * ROWS : i * SET + (w + 1) * ROWS]
+        to = outs[w].at[pl.ds(first, size)]
+        copies.append(pltpu.make_async_copy(total.at[w], to, sem.at[w]))
+        copies[-1].start()
+    for copy in copies:
+        copy.wait()
+
+
+def add_last(first, size, blocks, kept, got_p, got_m, grads):
     whole = pl.BlockSpec(kept.shape, lambda i: (0, 0))
-    step = math.gcd(first, size) if first else size
     hbm = pl.BlockSpec(memory_space=pl.ANY)
-    spec = pl.BlockSpec((step, ROWS, BLK), lambda i: (first // step + i, 0, 0))
-    part = pl.BlockSpec((step * SET, BLK), lambda i: (i, 0))
-    shape = jax.ShapeDtypeStruct((blocks, ROWS, BLK), F32)
     given = [] if grads is None else list(grads)
-    return call(
-        functools.partial(last_kernel, step), "add_last", (size // step,),
-        [part] * 3 + [hbm] * len(given), [spec] * 3, [shape] * 3,
-        (kept, got_p, got_m, *given), {3 + i: i for i in range(len(given))}, flops=flops,
-    )
+    return pl.pallas_call(
+        functools.partial(last_kernel, first, size),
+        grid=(1,),
+        in_specs=[whole] * 3 + [hbm] * len(given),
+        out_specs=[hbm] * 3,
+        out_shape=[jax.ShapeDtypeStruct((blocks, ROWS, BLK), F32)] * 3,
+        scratch_shapes=[
+            pltpu.VMEM((3, size, ROWS, BLK), F32),
+            pltpu.SemaphoreType.DMA((3,)),
+        ],
+        input_output_aliases={3 + i: i for i in range(len(given))},
+        compiler_params=pltpu.CompilerParams(vmem_limit_bytes=FULL_BYTES),
+        cost_estimate=pl.CostEstimate(flops=0, bytes_accessed=0, transcendentals=0),
+        name="add_last",
+    )(kept, got_p, got_m, *given)
 
 
 def body(tokens, grad_out, gate_weight, up_weight, down_weight, gate_index, up_index, down_index):
     row_count, width = tokens.shape
     scale = 1.0 / math.sqrt(row_count * lax.axis_size("dp"))
     me, flip = lax.axis_index("dp"), lax.rem(lax.axis_index("tensor"), 2)
-    place = jnp.stack([lax.rem(me, 4), lax.div(me, 4), flip]).astype(jnp.int32)
+    places = [
+        jnp.stack([lax.rem(me, 4), lax.div(me, 4), flip]).astype(jnp.int32)
+        for c in range(len(CHUNKS))
+    ]
     ids = (gate_index, up_index, down_index)
     weights = (gate_weight, up_weight, down_weight)
     blocks = gate_weight.shape[0]
 
-    def pairs(second, by):
+    def pairs(c, second, by):
         found = []
         for z in range(4):
             for y in range(4):
                 for t in range(8):
-                    along_y = (t % 2 == 0) != second
+                    along_y = t % 2 == (1 if second else 0)
                     to = (z, (y + by) % 4) if along_y else ((z + by) % 4, y)
                     found.append(((z * 4 + y) * 8 + t, (to[0] * 4 + to[1]) * 8 + t))
         return found
 
-    def send(up, down, second):
+    def send(c, up, down, second):
         axes = ("dp", "tensor")
         return (
-            lax.ppermute(up, axes, pairs(second, 1)),
-            lax.ppermute(down, axes, pairs(second, -1)),
+            lax.ppermute(up, axes, pairs(c, second, 1)),
+            lax.ppermute(down, axes, pairs(c, second, -1)),
         )
 
     starts = [sum(CHUNKS[:c]) for c in range(len(CHUNKS))]
@@ -340,35 +355,36 @@
     def chunk(c, *after):
         made.append(
             run_chunk(
-                starts[c], CHUNKS[c], scale, ids, place, tokens, grad_out, weights,
+                starts[c], CHUNKS[c], scale, ids, places[c], tokens, grad_out, weights,
                 made[-1][5:] if made else None, after,
             )
         )
 
-    def far(c, **order):
-        far_p, far_m, plus, minus = made[c][:4]
-        sent[c] = add_far(*send(far_p, far_m, False), plus, minus, **order)
+    def far(c, got, **order):
+        return add_far(*got, *made[c][2:4], **order)
 
     def near(c, **order):
-        sent[c] = add_near(made[c][4], *send(*sent[c], False), **order)
+        sent[c] = add_near(made[c][4], *send(c, *sent[c], False), **order)
 
     def far2(c, **order):
         far_p, far_m, plus, minus, kept = sent[c]
-        sent[c] = (*add_far2(*send(far_p, far_m, True), plus, minus, **order), kept)
-
-    def last(c, grads, flops=0):
+        sent[c] = (*add_far2(*send(c, far_p, far_m, True), plus, minus, **order), kept)
+
+    def last(c, grads):
         plus, minus, kept = sent[c]
-        return add_last(starts[c], CHUNKS[c], blocks, kept, *send(plus, minus, True), grads, flops)
+        return add_last(starts[c], CHUNKS[c], blocks, kept, *send(c, plus, minus, True), grads)
 
     chunk(0)
+    first = send(0, *made[0][:2], False)
     chunk(1)
-    far(0, after=(made[1][0],))
+    second = send(1, *made[1][:2], False)
+    sent[0] = far(0, first, after=(made[1][0],))
+    sent[1] = far(1, second, after=(sent[0][0],))
     partial, token = run_back(
-        ids[:2], *made[1][5:], gate_weight, up_weight, width, (sent[0][0],)
+        ids[:2], *made[1][5:], gate_weight, up_weight, width, (sent[0][0], sent[1][0])
     )
     summed = lax.psum_scatter(partial, "tensor", scatter_dimension=0, tiled=True)
-    far(1, after=(token,), flops=LONG)
-    near(0, after=(sent[1][0],))
+    near(0, after=(token,), flops=LONG)
     far2(0)
     near(1, after=(sent[0][0],))
     grads = last(0, grads)

time: 152 us -> 147 us (0.967)
  Pallas kernels: 92.4 us -> 89.2 us
  local copies, waits for them, and re-layouts: 3.67 us -> 2.09 us
    pallas_call x8 -> x6, Pallas kernels: 24.4 us -> 18.1 us  [call(): pl.pallas_call(run, grid=grid, in_specs=in_specs + [pl.BlockSpec(memory_s...]
    pallas_call x0 -> x2, Pallas kernels: none -> 4.58 us  [add_last(): pl.pallas_call(functools.partial(last_kernel, first, size), grid=(1,), in...]
    unnamed x20 -> x6, local copies, waits for them, and re-layouts: 3.67 us -> 2.09 us
    pallas_call x2, Pallas kernels: 45.6 us -> 44 us  [run_chunk(): pl.pallas_call(functools.partial(chunk_kernel, first, scale), grid_spec=p...]
  transfers between devices with their start and end apart: 17 -> 17, of which waited for: 6 -> 8; matrix products, arithmetic and copies ran while one was open for 0% -> 0% of each run, Pallas kernels for 44% -> 44%
where the time goes in v1:
time: 147 us; the launch traced here: 146 us
  Pallas kernels  89.2 us (61%)
  starting transfers between devices  27.6 us (19%)
  between operations  14.1 us (10%)
  waiting for transfers between devices  13.1 us (9%)
  local copies, waits for them, and re-layouts  2.09 us (1%)
    pallas_call x2, Pallas kernels, run_chunk(): pl.pallas_call(functools.partial(chunk_kernel, first, scale), grid_spec=p...  44 us
    pallas_call x1, Pallas kernels, run_back(): pl.pallas_call(kernel, grid_spec=pltpu.PrefetchScalarGridSpec(num_scalar_...  22.5 us
    ppermute x8, starting transfers between devices, send(): lax.ppermute(down, axes, pairs(c, second, -1))  18.7 us
    pallas_call x6, Pallas kernels, call(): pl.pallas_call(run, grid=grid, in_specs=in_specs + [pl.BlockSpec(memory_s...  18.1 us
    ppermute x8, waiting for transfers between devices, send(): lax.ppermute(up, axes, pairs(c, second, 1))  11.5 us
    ppermute x8, starting transfers between devices, send(): lax.ppermute(up, axes, pairs(c, second, 1))  8.8 us
    pallas_call x2, Pallas kernels, add_last(): pl.pallas_call(functools.partial(last_kernel, first, size), grid=(1,), in...  4.58 us
  transfers between devices with their start and end apart: 17, of which 8 were waited for; matrix products, arithmetic and copies ran while one was open for 0% of the time, Pallas kernels for 44%

profile of v1, /device:TPU:0, one launch (start us, length us, event | category | flops | bytes accessed | tf_op | source)
XLA Modules:
  0.0 146.1 jit_solution(12489684399582343209)
XLA Ops:
  7.2 0.0 reduce-scatter.2.cloned.1.call-start
  7.2 0.1 pad_add_fusion.place
  7.3 0.7 copy-done
  8.0 0.7 copy-done.1
  8.7 0.7 copy-done.2
  9.4 24.6 %chunk.2 = (bf16[2,2016,128]{2,1,0:T(8,128)(2,1)}, bf16[2,2016,128]{2,1,0:T(8,128)(2,1)}, bf16[4,2016,128]{2,1,0:T(8,128)(2,1)}, bf16[4,2016,128]{2,1,0:T(8,128)...) custom-call(s32[12,12]{1,0:T(8,128)S(1)} %copy-done.1, ...), custom_call_target="tpu_custom_call" | custom-call | flops 24999999488 | bytes 20971520 | tf_op jit(solution)/shard_map/chunk/pallas_call | solution.py:122
  34.0 1.7 %collective-permute-start = (bf16[2,2016,128]{2,1,0:T(8,128)(2,1)}, bf16[2,2016,128]{2,1,0:T(8,128)(2,1)}, u32[]{:S(2)}, u32[]{:S(2)}) collective-permute-start(bf16[2,2016,128]{2,1,0:T(8,128)(2,1)} %get-tuple-element.48), channel_id=1, source_target_pairs={{0,8},{1,33},{2,10},{3,35},{4,12},{5,37},{6,14},{7,39},{8,16},{9,4... | collective-permute-start | bytes 3096584 | tf_op jit(solution)/shard_map/ppermute | solution.py:348
  35.7 1.6 %collective-permute-start.1 = (bf16[2,2016,128]{2,1,0:T(8,128)(2,1)}, bf16[2,2016,128]{2,1,0:T(8,128)(2,1)}, u32[]{:S(2)}, u32[]{:S(2)}) collective-permute-start(bf16[2,2016,128]{2,1,0:T(8,128)(2,1)} %get-tuple-element.49), channel_id=1, source_target_pairs={{0,24},{1,97},{2,26},{3,99},{4,28},{5,101},{6,30},{7,103},{8,0},{9... | collective-permute-start | bytes 3096584 | tf_op jit(solution)/shard_map/ppermute | solution.py:349
  37.3 19.4 %chunk.3 = (bf16[2,1440,128]{2,1,0:T(8,128)(2,1)}, bf16[2,1440,128]{2,1,0:T(8,128)(2,1)}, bf16[4,1440,128]{2,1,0:T(8,128)(2,1)}, bf16[4,1440,128]{2,1,0:T(8,128)...) custom-call(s32[12,12]{1,0:T(8,128)S(1)} %copy-done.1, ...), custom_call_target="tpu_custom_call", output_to_operand_aliasing={{5}: (9, {}), {6}: (10, {})} | custom-call | flops 24999999488 | bytes 20971520 | tf_op jit(solution)/shard_map/chunk/pallas_call | solution.py:122
  56.7 0.5 collective-permute-start.2
  57.2 2.8 %collective-permute-start.3 = (bf16[2,1440,128]{2,1,0:T(8,128)(2,1)}, bf16[2,1440,128]{2,1,0:T(8,128)(2,1)}, u32[]{:S(2)}, u32[]{:S(2)}) collective-permute-start(bf16[2,1440,128]{2,1,0:T(8,128)(2,1)} %get-tuple-element.54), channel_id=1, source_target_pairs={{0,24},{1,97},{2,26},{3,99},{4,28},{5,101},{6,30},{7,103},{8,0},{9... | collective-permute-start | bytes 2211848 | tf_op jit(solution)/shard_map/ppermute | solution.py:349
  60.0 0.0 collective-permute-done.refs_0_
  60.0 0.0 collective-permute-done.1.refs_1_
  60.0 3.3 %add_far.2 = (bf16[4,2016,128]{2,1,0:T(8,128)(2,1)}, bf16[4,2016,128]{2,1,0:T(8,128)(2,1)}) custom-call(bf16[2,2016,128]{2,1,0:T(8,128)(2,1)} %collective-permute-done.refs_0_, bf16[2,2016,128]{2,1,0:T(8,128)(2,1)} %collective-permute-done.1.refs_1_, bf16[4,2016,128]{2,1,0:T(8,128)(2,1)} %get-tuple-element.50.refs_2_, ...), custom_call_target="tpu_custom_call", output_to_operand_aliasing={{0}: (2, {}), {1}: (3, {})} | custom-call | tf_op jit(solution)/shard_map/add_far/pallas_call | solution.py:219
  63.2 0.0 collective-permute-start.6
  63.2 3.2 %collective-permute-start.7 = (bf16[4,2016,128]{2,1,0:T(8,128)(2,1)}, bf16[4,2016,128]{2,1,0:T(8,128)(2,1)}, u32[]{:S(2)}, u32[]{:S(2)}) collective-permute-start(bf16[4,2016,128]{2,1,0:T(8,128)(2,1)} %get-tuple-element.62), channel_id=1, source_target_pairs={{0,24},{1,97},{2,26},{3,99},{4,28},{5,101},{6,30},{7,103},{8,0},{9... | collective-permute-start | bytes 6193160 | tf_op jit(solution)/shard_map/ppermute | solution.py:349
  66.5 3.2 %collective-permute-done.2.refs_0_ = bf16[2,1440,128]{2,1,0:T(8,128)(2,1)} collective-permute-done((bf16[2,1440,128]{2,1,0:T(8,128)(2,1)}, bf16[2,1440,128]{2,1,0:T(8,128)(2,1)}, u32[]{:S(2)}, u32[]{:S(2)}) %collective-permute-start.2) | collective-permute-done | bytes 737312 | tf_op jit(solution)/shard_map/ppermute | solution.py:348
  69.7 0.0 collective-permute-done.3.refs_1_
  69.7 2.8 %add_far.3 = (bf16[4,1440,128]{2,1,0:T(8,128)(2,1)}, bf16[4,1440,128]{2,1,0:T(8,128)(2,1)}) custom-call(bf16[2,1440,128]{2,1,0:T(8,128)(2,1)} %collective-permute-done.2.refs_0_, bf16[2,1440,128]{2,1,0:T(8,128)(2,1)} %collective-permute-done.3.refs_1_, ...), custom_call_target="tpu_custom_call", output_to_operand_aliasing={{0}: (2, {}), {1}: (3, {})} | custom-call | tf_op jit(solution)/shard_map/add_far/pallas_call | solution.py:219
  72.5 0.8 collective-permute-start.4
  73.3 2.5 %collective-permute-start.5 = (bf16[4,1440,128]{2,1,0:T(8,128)(2,1)}, bf16[4,1440,128]{2,1,0:T(8,128)(2,1)}, u32[]{:S(2)}, u32[]{:S(2)}) collective-permute-start(bf16[4,1440,128]{2,1,0:T(8,128)(2,1)} %get-tuple-element.60), channel_id=1, source_target_pairs={{0,24},{1,97},{2,26},{3,99},{4,28},{5,101},{6,30},{7,103},{8,0},{9... | collective-permute-start | bytes 4423688 | tf_op jit(solution)/shard_map/ppermute | solution.py:349
  75.8 22.5 %back.1 = (bf16[384,6144]{1,0:T(8,128)(2,1)}, f32[8,128]{1,0:T(8,128)}) custom-call(s32[12,12]{1,0:T(8,128)} %refs_0_.1, s32[12,12]{1,0:T(8,128)} %refs_1_.1, bf16[384,1536]{1,0:T(8,128)(2,1)} %get-tuple-element.46.refs_2_, bf16[384,1536]{1,0:T(8,128)(2,1)} %get-tuple-element.47.refs_3_, bf16[12,12,128,128]{3,2,1,0:T(8,128)(2,1)} %refs_4_.1, ...), custom_call_target="tpu_custom_call" | custom-call | flops 24999999488 | bytes 16777216 | tf_op jit(solution)/shard_map/back/pallas_call | solution.py:184
  98.3 0.0 reduce-scatter.2.cloned.1.call-update
  98.3 0.0 collective-permute-done.6.refs_1_
  98.3 4.3 %add_near.2 = (bf16[1008,128]{1,0:T(8,128)(2,1)}, bf16[1008,128]{1,0:T(8,128)(2,1)}, bf16[2016,128]{1,0:T(8,128)(2,1)}, bf16[2016,128]{1,0:T(8,128)(2,1)}, bf16[2016,128]{1,0:T(8,128)(2,1)}) custom-call(bf16[4,2016,128]{2,1,0:T(8,128)(2,1)} %get-tuple-element.61.refs_0_, bf16[4,2016,128]{2,1,0:T(8,128)(2,1)} %collective-permute-done.6.refs_1_, ...), custom_call_target="tpu_custom_call" | custom-call | flops 199999995904 | tf_op jit(solution)/shard_map/add_near/pallas_call | solution.py:219
  102.6 2.0 %collective-permute-start.8 = (bf16[1008,128]{1,0:T(8,128)(2,1)}, bf16[1008,128]{1,0:T(8,128)(2,1)}, u32[]{:S(2)}, u32[]{:S(2)}) collective-permute-start(bf16[1008,128]{1,0:T(8,128)(2,1)} %get-tuple-element.64), channel_id=1, source_target_pairs={{0,32},{1,9},{2,34},{3,11},{4,36},{5,13},{6,38},{7,15},{8,40},{9,1... | collective-permute-start | bytes 774152 | tf_op jit(solution)/shard_map/ppermute | solution.py:348
  104.6 2.4 %collective-permute-start.9 = (bf16[1008,128]{1,0:T(8,128)(2,1)}, bf16[1008,128]{1,0:T(8,128)(2,1)}, u32[]{:S(2)}, u32[]{:S(2)}) collective-permute-start(bf16[1008,128]{1,0:T(8,128)(2,1)} %get-tuple-element.65), channel_id=1, source_target_pairs={{0,96},{1,25},{2,98},{3,27},{4,100},{5,29},{6,102},{7,31},{8,104},... | collective-permute-start | bytes 774152 | tf_op jit(solution)/shard_map/ppermute | solution.py:349
  107.0 4.4 %collective-permute-done.8.refs_0_ = bf16[1008,128]{1,0:T(8,128)(2,1)} collective-permute-done((bf16[1008,128]{1,0:T(8,128)(2,1)}, bf16[1008,128]{1,0:T(8,128)(2,1)}, u32[]{:S(2)}, u32[]{:S(2)}) %collective-permute-start.8) | collective-permute-done | bytes 258080 | tf_op jit(solution)/shard_map/ppermute | solution.py:348
  111.4 2.2 %add_far2.2 = (bf16[2016,128]{1,0:T(8,128)(2,1)}, bf16[2016,128]{1,0:T(8,128)(2,1)}) custom-call(bf16[1008,128]{1,0:T(8,128)(2,1)} %collective-permute-done.8.refs_0_, bf16[1008,128]{1,0:T(8,128)(2,1)} %collective-permute-done.9.refs_1_, bf16[2016,128]{1,0:T(8,128)(2,1)} %get-tuple-element.66.refs_2_, ...), custom_call_target="tpu_custom_call", output_to_operand_aliasing={{0}: (2, {}), {1}: (3, {})} | custom-call | tf_op jit(solution)/shard_map/add_far2/pallas_call | solution.py:219
  113.6 0.0 collective-permute-done.4.refs_1_
  113.6 0.0 collective-permute-done.5.refs_2_
  113.6 3.6 %add_near.3 = (bf16[720,128]{1,0:T(8,128)(2,1)}, bf16[720,128]{1,0:T(8,128)(2,1)}, bf16[1440,128]{1,0:T(8,128)(2,1)}, bf16[1440,128]{1,0:T(8,128)(2,1)}, bf16[1440,128]{1,0:T(8,128)(2,1)}) custom-call(bf16[4,1440,128]{2,1,0:T(8,128)(2,1)} %get-tuple-element.59.refs_0_, bf16[4,1440,128]{2,1,0:T(8,128)(2,1)} %collective-permute-done.4.refs_1_, ...), custom_call_target="tpu_custom_call" | custom-call | tf_op jit(solution)/shard_map/add_near/pallas_call | solution.py:219
  117.2 1.8 %collective-permute-start.10 = (bf16[720,128]{1,0:T(8,128)(2,1)}, bf16[720,128]{1,0:T(8,128)(2,1)}, u32[]{:S(2)}, u32[]{:S(2)}) collective-permute-start(bf16[720,128]{1,0:T(8,128)(2,1)} %get-tuple-element.70), channel_id=1, source_target_pairs={{0,32},{1,9},{2,34},{3,11},{4,36},{5,13},{6,38},{7,15},{8,40},{9,1... | collective-permute-start | bytes 552968 | tf_op jit(solution)/shard_map/ppermute | solution.py:348
  119.0 1.7 %collective-permute-start.11 = (bf16[720,128]{1,0:T(8,128)(2,1)}, bf16[720,128]{1,0:T(8,128)(2,1)}, u32[]{:S(2)}, u32[]{:S(2)}) collective-permute-start(bf16[720,128]{1,0:T(8,128)(2,1)} %get-tuple-element.71), channel_id=1, source_target_pairs={{0,96},{1,25},{2,98},{3,27},{4,100},{5,29},{6,102},{7,31},{8,104},... | collective-permute-start | bytes 552968 | tf_op jit(solution)/shard_map/ppermute | solution.py:349
  120.7 0.3 collective-permute-start.14
  121.0 2.9 %collective-permute-start.15 = (bf16[2016,128]{1,0:T(8,128)(2,1)}, bf16[2016,128]{1,0:T(8,128)(2,1)}, u32[]{:S(2)}, u32[]{:S(2)}) collective-permute-start(bf16[2016,128]{1,0:T(8,128)(2,1)} %get-tuple-element.77), channel_id=1, source_target_pairs={{0,96},{1,25},{2,98},{3,27},{4,100},{5,29},{6,102},{7,31},{8,104},... | collective-permute-start | bytes 1548296 | tf_op jit(solution)/shard_map/ppermute | solution.py:349
  123.9 0.5 collective-permute-done.10.refs_0_
  124.5 0.4 collective-permute-done.11.refs_1_
  124.8 2.0 %add_far2.3 = (bf16[1440,128]{1,0:T(8,128)(2,1)}, bf16[1440,128]{1,0:T(8,128)(2,1)}) custom-call(bf16[720,128]{1,0:T(8,128)(2,1)} %collective-permute-done.10.refs_0_, bf16[720,128]{1,0:T(8,128)(2,1)} %collective-permute-done.11.refs_1_, bf16[1440,128]{1,0:T(8,128)(2,1)} %get-tuple-element.72.refs_2_, ...), custom_call_target="tpu_custom_call", output_to_operand_aliasing={{0}: (2, {}), {1}: (3, {})} | custom-call | tf_op jit(solution)/shard_map/add_far2/pallas_call | solution.py:219
  126.8 1.6 %collective-permute-start.12 = (bf16[1440,128]{1,0:T(8,128)(2,1)}, bf16[1440,128]{1,0:T(8,128)(2,1)}, u32[]{:S(2)}, u32[]{:S(2)}) collective-permute-start(bf16[1440,128]{1,0:T(8,128)(2,1)} %get-tuple-element.74), channel_id=1, source_target_pairs={{0,32},{1,9},{2,34},{3,11},{4,36},{5,13},{6,38},{7,15},{8,40},{9,1... | collective-permute-start | bytes 1105928 | tf_op jit(solution)/shard_map/ppermute | solution.py:348
  128.5 1.6 %collective-permute-start.13 = (bf16[1440,128]{1,0:T(8,128)(2,1)}, bf16[1440,128]{1,0:T(8,128)(2,1)}, u32[]{:S(2)}, u32[]{:S(2)}) collective-permute-start(bf16[1440,128]{1,0:T(8,128)(2,1)} %get-tuple-element.75), channel_id=1, source_target_pairs={{0,96},{1,25},{2,98},{3,27},{4,100},{5,29},{6,102},{7,31},{8,104},... | collective-permute-start | bytes 1105928 | tf_op jit(solution)/shard_map/ppermute | solution.py:349
  130.1 1.2 collective-permute-done.14.got_p
  131.3 0.0 collective-permute-done.15.got_m
  131.3 2.4 %add_last.2 = (f32[12,96,128]{2,1,0:T(8,128)}, f32[12,96,128]{2,1,0:T(8,128)}, f32[12,96,128]{2,1,0:T(8,128)}) custom-call(bf16[2016,128]{1,0:T(8,128)(2,1)} %get-tuple-element.76.kept, bf16[2016,128]{1,0:T(8,128)(2,1)} %collective-permute-done.14.got_p, bf16[2016,128]{1,0:T(8,128)(2,1)} %collective-permute-done.15.got_m), custom_call_target="tpu_custom_call" | custom-call | tf_op jit(solution)/shard_map/add_last/pallas_call | solution.py:306
  133.8 2.1 %collective-permute-done.12.got_p = bf16[1440,128]{1,0:T(8,128)(2,1)} collective-permute-done((bf16[1440,128]{1,0:T(8,128)(2,1)}, bf16[1440,128]{1,0:T(8,128)(2,1)}, u32[]{:S(2)}, u32[]{:S(2)}) %collective-permute-start.12) | collective-permute-done | bytes 368672 | tf_op jit(solution)/shard_map/ppermute | solution.py:348
  135.9 0.4 collective-permute-done.13.got_m
  136.3 2.2 %add_last.3 = (f32[12,96,128]{2,1,0:T(8,128)}, f32[12,96,128]{2,1,0:T(8,128)}, f32[12,96,128]{2,1,0:T(8,128)}) custom-call(bf16[1440,128]{1,0:T(8,128)(2,1)} %get-tuple-element.69.kept, bf16[1440,128]{1,0:T(8,128)(2,1)} %collective-permute-done.12.got_p, ...), custom_call_target="tpu_custom_call", output_to_operand_aliasing={{0}: (3, {}), {1}: (4, {}), {2}: (5, {})} | custom-call | tf_op jit(solution)/shard_map/add_last/pallas_call | solution.py:306
  138.5 0.8 reduce-scatter.2.cloned.1.call-done
  (5 shorter events, 0.0 us)
Async XLA Ops:
  7.2 132.0 %reduce-scatter.2.cloned.1.call-start = ((), (), s32[]{:S(2)}) async-start(), calls=%async_computation.1 | async-start | bytes 5308416 | tf_op jit(solution)/shard_map/reduce_scatter | solution.py:386
  7.3 0.7 copy-start
  8.0 0.7 copy-start.1
  8.7 0.7 copy-start.2
  34.0 26.0 %collective-permute-start = (bf16[2,2016,128]{2,1,0:T(8,128)(2,1)}, bf16[2,2016,128]{2,1,0:T(8,128)(2,1)}, u32[]{:S(2)}, u32[]{:S(2)}) collective-permute-start(bf16[2,2016,128]{2,1,0:T(8,128)(2,1)} %get-tuple-element.48), channel_id=1, source_target_pairs={{0,8},{1,33},{2,10},{3,35},{4,12},{5,37},{6,14},{7,39},{8,16},{9,4... | collective-permute-start | bytes 3096584 | tf_op jit(solution)/shard_map/ppermute | solution.py:348
  35.7 24.3 %collective-permute-start.1 = (bf16[2,2016,128]{2,1,0:T(8,128)(2,1)}, bf16[2,2016,128]{2,1,0:T(8,128)(2,1)}, u32[]{:S(2)}, u32[]{:S(2)}) collective-permute-start(bf16[2,2016,128]{2,1,0:T(8,128)(2,1)} %get-tuple-element.49), channel_id=1, source_target_pairs={{0,24},{1,97},{2,26},{3,99},{4,28},{5,101},{6,30},{7,103},{8,0},{9... | collective-permute-start | bytes 3096584 | tf_op jit(solution)/shard_map/ppermute | solution.py:349
  56.7 13.0 %collective-permute-start.2 = (bf16[2,1440,128]{2,1,0:T(8,128)(2,1)}, bf16[2,1440,128]{2,1,0:T(8,128)(2,1)}, u32[]{:S(2)}, u32[]{:S(2)}) collective-permute-start(bf16[2,1440,128]{2,1,0:T(8,128)(2,1)} %get-tuple-element.52.refs_4_), channel_id=1, source_target_pairs={{0,8},{1,33},{2,10},{3,35},{4,12},{5,37},{6,14},{7,39},{8,16},{9,4... | collective-permute-start | bytes 2211848 | tf_op jit(solution)/shard_map/ppermute | solution.py:348
  57.2 12.5 %collective-permute-start.3 = (bf16[2,1440,128]{2,1,0:T(8,128)(2,1)}, bf16[2,1440,128]{2,1,0:T(8,128)(2,1)}, u32[]{:S(2)}, u32[]{:S(2)}) collective-permute-start(bf16[2,1440,128]{2,1,0:T(8,128)(2,1)} %get-tuple-element.54), channel_id=1, source_target_pairs={{0,24},{1,97},{2,26},{3,99},{4,28},{5,101},{6,30},{7,103},{8,0},{9... | collective-permute-start | bytes 2211848 | tf_op jit(solution)/shard_map/ppermute | solution.py:349
  63.2 35.0 %collective-permute-start.6 = (bf16[4,2016,128]{2,1,0:T(8,128)(2,1)}, bf16[4,2016,128]{2,1,0:T(8,128)(2,1)}, u32[]{:S(2)}, u32[]{:S(2)}) collective-permute-start(bf16[4,2016,128]{2,1,0:T(8,128)(2,1)} %get-tuple-element.53.refs_4_.refs_6_), channel_id=1, source_target_pairs={{0,8},{1,33},{2,10},{3,35},{4,12},{5,37},{6,14},{7,39},{8,16},{9,4... | collective-permute-start | bytes 6193160 | tf_op jit(solution)/shard_map/ppermute | solution.py:348
  63.2 35.0 %collective-permute-start.7 = (bf16[4,2016,128]{2,1,0:T(8,128)(2,1)}, bf16[4,2016,128]{2,1,0:T(8,128)(2,1)}, u32[]{:S(2)}, u32[]{:S(2)}) collective-permute-start(bf16[4,2016,128]{2,1,0:T(8,128)(2,1)} %get-tuple-element.62), channel_id=1, source_target_pairs={{0,24},{1,97},{2,26},{3,99},{4,28},{5,101},{6,30},{7,103},{8,0},{9... | collective-permute-start | bytes 6193160 | tf_op jit(solution)/shard_map/ppermute | solution.py:349
  72.5 41.1 %collective-permute-start.4 = (bf16[4,1440,128]{2,1,0:T(8,128)(2,1)}, bf16[4,1440,128]{2,1,0:T(8,128)(2,1)}, u32[]{:S(2)}, u32[]{:S(2)}) collective-permute-start(bf16[4,1440,128]{2,1,0:T(8,128)(2,1)} %get-tuple-element.57.refs_7_), channel_id=1, source_target_pairs={{0,8},{1,33},{2,10},{3,35},{4,12},{5,37},{6,14},{7,39},{8,16},{9,4... | collective-permute-start | bytes 4423688 | tf_op jit(solution)/shard_map/ppermute | solution.py:348
  73.3 40.3 %collective-permute-start.5 = (bf16[4,1440,128]{2,1,0:T(8,128)(2,1)}, bf16[4,1440,128]{2,1,0:T(8,128)(2,1)}, u32[]{:S(2)}, u32[]{:S(2)}) collective-permute-start(bf16[4,1440,128]{2,1,0:T(8,128)(2,1)} %get-tuple-element.60), channel_id=1, source_target_pairs={{0,24},{1,97},{2,26},{3,99},{4,28},{5,101},{6,30},{7,103},{8,0},{9... | collective-permute-start | bytes 4423688 | tf_op jit(solution)/shard_map/ppermute | solution.py:349
  102.6 8.8 %collective-permute-start.8 = (bf16[1008,128]{1,0:T(8,128)(2,1)}, bf16[1008,128]{1,0:T(8,128)(2,1)}, u32[]{:S(2)}, u32[]{:S(2)}) collective-permute-start(bf16[1008,128]{1,0:T(8,128)(2,1)} %get-tuple-element.64), channel_id=1, source_target_pairs={{0,32},{1,9},{2,34},{3,11},{4,36},{5,13},{6,38},{7,15},{8,40},{9,1... | collective-permute-start | bytes 774152 | tf_op jit(solution)/shard_map/ppermute | solution.py:348
  104.6 6.7 %collective-permute-start.9 = (bf16[1008,128]{1,0:T(8,128)(2,1)}, bf16[1008,128]{1,0:T(8,128)(2,1)}, u32[]{:S(2)}, u32[]{:S(2)}) collective-permute-start(bf16[1008,128]{1,0:T(8,128)(2,1)} %get-tuple-element.65), channel_id=1, source_target_pairs={{0,96},{1,25},{2,98},{3,27},{4,100},{5,29},{6,102},{7,31},{8,104},... | collective-permute-start | bytes 774152 | tf_op jit(solution)/shard_map/ppermute | solution.py:349
  117.2 7.3 %collective-permute-start.10 = (bf16[720,128]{1,0:T(8,128)(2,1)}, bf16[720,128]{1,0:T(8,128)(2,1)}, u32[]{:S(2)}, u32[]{:S(2)}) collective-permute-start(bf16[720,128]{1,0:T(8,128)(2,1)} %get-tuple-element.70), channel_id=1, source_target_pairs={{0,32},{1,9},{2,34},{3,11},{4,36},{5,13},{6,38},{7,15},{8,40},{9,1... | collective-permute-start | bytes 552968 | tf_op jit(solution)/shard_map/ppermute | solution.py:348
  119.0 5.9 %collective-permute-start.11 = (bf16[720,128]{1,0:T(8,128)(2,1)}, bf16[720,128]{1,0:T(8,128)(2,1)}, u32[]{:S(2)}, u32[]{:S(2)}) collective-permute-start(bf16[720,128]{1,0:T(8,128)(2,1)} %get-tuple-element.71), channel_id=1, source_target_pairs={{0,96},{1,25},{2,98},{3,27},{4,100},{5,29},{6,102},{7,31},{8,104},... | collective-permute-start | bytes 552968 | tf_op jit(solution)/shard_map/ppermute | solution.py:349
  120.7 10.6 %collective-permute-start.14 = (bf16[2016,128]{1,0:T(8,128)(2,1)}, bf16[2016,128]{1,0:T(8,128)(2,1)}, u32[]{:S(2)}, u32[]{:S(2)}) collective-permute-start(bf16[2016,128]{1,0:T(8,128)(2,1)} %get-tuple-element.68.refs_3_), channel_id=1, source_target_pairs={{0,32},{1,9},{2,34},{3,11},{4,36},{5,13},{6,38},{7,15},{8,40},{9,1... | collective-permute-start | bytes 1548296 | tf_op jit(solution)/shard_map/ppermute | solution.py:348
  121.0 10.3 %collective-permute-start.15 = (bf16[2016,128]{1,0:T(8,128)(2,1)}, bf16[2016,128]{1,0:T(8,128)(2,1)}, u32[]{:S(2)}, u32[]{:S(2)}) collective-permute-start(bf16[2016,128]{1,0:T(8,128)(2,1)} %get-tuple-element.77), channel_id=1, source_target_pairs={{0,96},{1,25},{2,98},{3,27},{4,100},{5,29},{6,102},{7,31},{8,104},... | collective-permute-start | bytes 1548296 | tf_op jit(solution)/shard_map/ppermute | solution.py:349
  126.8 9.0 %collective-permute-start.12 = (bf16[1440,128]{1,0:T(8,128)(2,1)}, bf16[1440,128]{1,0:T(8,128)(2,1)}, u32[]{:S(2)}, u32[]{:S(2)}) collective-permute-start(bf16[1440,128]{1,0:T(8,128)(2,1)} %get-tuple-element.74), channel_id=1, source_target_pairs={{0,32},{1,9},{2,34},{3,11},{4,36},{5,13},{6,38},{7,15},{8,40},{9,1... | collective-permute-start | bytes 1105928 | tf_op jit(solution)/shard_map/ppermute | solution.py:348
  128.5 7.8 %collective-permute-start.13 = (bf16[1440,128]{1,0:T(8,128)(2,1)}, bf16[1440,128]{1,0:T(8,128)(2,1)}, u32[]{:S(2)}, u32[]{:S(2)}) collective-permute-start(bf16[1440,128]{1,0:T(8,128)(2,1)} %get-tuple-element.75), channel_id=1, source_target_pairs={{0,96},{1,25},{2,98},{3,27},{4,100},{5,29},{6,102},{7,31},{8,104},... | collective-permute-start | bytes 1105928 | tf_op jit(solution)/shard_map/ppermute | solution.py:349
Sparse Core Ops, SparseCore 0:
  98.4 40.7 reduce-scatter.1

commit v2 on v1

--- a/solution.py
+++ b/solution.py
@@ -83,19 +83,21 @@
             at = jnp.where(flip == 0, y_rel * 4 + z_rel, z_rel * 4 + y_rel)
             terms[at, w * ROWS : (w + 1) * ROWS] = term[shard * ROWS : (shard + 1) * ROWS]
 
-    for z_rel in range(4):
-        group = 3 * lax.rem(z + z_rel, 4)
-        wide = []
-        for left, source, ids in (
-            (gate_t, tok, gate_ids), (up_t, tok, up_ids), (hidden_t, out_grad, down_ids)
+    cut = 2 * BLK
+    for z_first in (0, 2):
+        groups = [3 * lax.rem(z + z_first + n, 4) for n in range(2)]
+        for w, (left, source, ids) in enumerate(
+            ((gate_t, tok, gate_ids), (up_t, tok, up_ids), (hidden_t, out_grad, down_ids))
         ):
             right = jnp.concatenate(
-                [block_at(source, ids[j, group + i]) for i in range(3)], axis=1
+                [block_at(source, ids[j, g + i]) for g in groups for i in range(3)], axis=1
             )
-            wide.append((dot(left, right) * scale).astype(BF))
-        for w, term in enumerate(wide):
-            parts = [term[:, i * BLK : (i + 1) * BLK] for i in range(3)]
-            put(z_rel, w, jnp.concatenate(parts if w == 2 else [p.T for p in parts], axis=0))
+            wide = dot(left[:, :cut], right[:cut]) + dot(left[:, cut:], right[cut:])
+            wide = (wide * scale).astype(BF)
+            for n in range(2):
+                parts = [wide[:, i * BLK : (i + 1) * BLK] for i in range(3 * n, 3 * n + 3)]
+                parts = parts if w == 2 else [p.T for p in parts]
+                put(z_first + n, w, jnp.concatenate(parts, axis=0))
 
     own[...] = terms[0:4]
     plus[...] = terms[4:8]

time: 147 us -> 146 us (level)
  no operation moved by 1% of the time
where the time goes in v2:
time: 146 us; the launch traced here: 145 us
  Pallas kernels  88.4 us (61%)
  starting transfers between devices  27.5 us (19%)
  between operations  14.1 us (10%)
  waiting for transfers between devices  13.1 us (9%)
  local copies, waits for them, and re-layouts  2.09 us (1%)
    pallas_call x2, Pallas kernels, run_chunk(): pl.pallas_call(functools.partial(chunk_kernel, first, scale), grid_spec=p...  43.3 us
    pallas_call x1, Pallas kernels, run_back(): pl.pallas_call(kernel, grid_spec=pltpu.PrefetchScalarGridSpec(num_scalar_...  22.5 us
    ppermute x8, starting transfers between devices, send(): lax.ppermute(down, axes, pairs(c, second, -1))  18.6 us
    pallas_call x6, Pallas kernels, call(): pl.pallas_call(run, grid=grid, in_specs=in_specs + [pl.BlockSpec(memory_s...  18.1 us
    ppermute x8, waiting for transfers between devices, send(): lax.ppermute(up, axes, pairs(c, second, 1))  11.5 us
    ppermute x8, starting transfers between devices, send(): lax.ppermute(up, axes, pairs(c, second, 1))  8.91 us
    pallas_call x2, Pallas kernels, add_last(): pl.pallas_call(functools.partial(last_kernel, first, size), grid=(1,), in...  4.58 us
  transfers between devices with their start and end apart: 17, of which 8 were waited for; matrix products, arithmetic and copies ran while one was open for 0% of the time, Pallas kernels for 44%

profile of v2, /device:TPU:0, one launch (start us, length us, event | category | flops | bytes accessed | tf_op | source)
XLA Modules:
  0.0 145.4 jit_solution(11308247775988987068)
XLA Ops:
  7.2 0.0 reduce-scatter.2.cloned.1.call-start
  7.2 0.1 pad_add_fusion.place
  7.3 0.7 copy-done
  8.0 0.7 copy-done.1
  8.7 0.7 copy-done.2
  9.4 24.2 %chunk.2 = (bf16[2,2016,128]{2,1,0:T(8,128)(2,1)}, bf16[2,2016,128]{2,1,0:T(8,128)(2,1)}, bf16[4,2016,128]{2,1,0:T(8,128)(2,1)}, bf16[4,2016,128]{2,1,0:T(8,128)...) custom-call(s32[12,12]{1,0:T(8,128)S(1)} %copy-done.1, ...), custom_call_target="tpu_custom_call" | custom-call | flops 24999999488 | bytes 20971520 | tf_op jit(solution)/shard_map/chunk/pallas_call | solution.py:124
  33.6 1.7 %collective-permute-start = (bf16[2,2016,128]{2,1,0:T(8,128)(2,1)}, bf16[2,2016,128]{2,1,0:T(8,128)(2,1)}, u32[]{:S(2)}, u32[]{:S(2)}) collective-permute-start(bf16[2,2016,128]{2,1,0:T(8,128)(2,1)} %get-tuple-element.48), channel_id=1, source_target_pairs={{0,8},{1,33},{2,10},{3,35},{4,12},{5,37},{6,14},{7,39},{8,16},{9,4... | collective-permute-start | bytes 3096584 | tf_op jit(solution)/shard_map/ppermute | solution.py:350
  35.3 1.6 %collective-permute-start.1 = (bf16[2,2016,128]{2,1,0:T(8,128)(2,1)}, bf16[2,2016,128]{2,1,0:T(8,128)(2,1)}, u32[]{:S(2)}, u32[]{:S(2)}) collective-permute-start(bf16[2,2016,128]{2,1,0:T(8,128)(2,1)} %get-tuple-element.49), channel_id=1, source_target_pairs={{0,24},{1,97},{2,26},{3,99},{4,28},{5,101},{6,30},{7,103},{8,0},{9... | collective-permute-start | bytes 3096584 | tf_op jit(solution)/shard_map/ppermute | solution.py:351
  36.9 19.1 %chunk.3 = (bf16[2,1440,128]{2,1,0:T(8,128)(2,1)}, bf16[2,1440,128]{2,1,0:T(8,128)(2,1)}, bf16[4,1440,128]{2,1,0:T(8,128)(2,1)}, bf16[4,1440,128]{2,1,0:T(8,128)...) custom-call(s32[12,12]{1,0:T(8,128)S(1)} %copy-done.1, ...), custom_call_target="tpu_custom_call", output_to_operand_aliasing={{5}: (9, {}), {6}: (10, {})} | custom-call | flops 24999999488 | bytes 20971520 | tf_op jit(solution)/shard_map/chunk/pallas_call | solution.py:124
  55.9 0.5 collective-permute-start.2
  56.5 2.8 %collective-permute-start.3 = (bf16[2,1440,128]{2,1,0:T(8,128)(2,1)}, bf16[2,1440,128]{2,1,0:T(8,128)(2,1)}, u32[]{:S(2)}, u32[]{:S(2)}) collective-permute-start(bf16[2,1440,128]{2,1,0:T(8,128)(2,1)} %get-tuple-element.54), channel_id=1, source_target_pairs={{0,24},{1,97},{2,26},{3,99},{4,28},{5,101},{6,30},{7,103},{8,0},{9... | collective-permute-start | bytes 2211848 | tf_op jit(solution)/shard_map/ppermute | solution.py:351
  59.2 0.0 collective-permute-done.refs_0_
  59.2 0.0 collective-permute-done.1.refs_1_
  59.2 3.3 %add_far.2 = (bf16[4,2016,128]{2,1,0:T(8,128)(2,1)}, bf16[4,2016,128]{2,1,0:T(8,128)(2,1)}) custom-call(bf16[2,2016,128]{2,1,0:T(8,128)(2,1)} %collective-permute-done.refs_0_, bf16[2,2016,128]{2,1,0:T(8,128)(2,1)} %collective-permute-done.1.refs_1_, bf16[4,2016,128]{2,1,0:T(8,128)(2,1)} %get-tuple-element.50.refs_2_, ...), custom_call_target="tpu_custom_call", output_to_operand_aliasing={{0}: (2, {}), {1}: (3, {})} | custom-call | tf_op jit(solution)/shard_map/add_far/pallas_call | solution.py:221
  62.5 0.0 collective-permute-start.6
  62.5 3.2 %collective-permute-start.7 = (bf16[4,2016,128]{2,1,0:T(8,128)(2,1)}, bf16[4,2016,128]{2,1,0:T(8,128)(2,1)}, u32[]{:S(2)}, u32[]{:S(2)}) collective-permute-start(bf16[4,2016,128]{2,1,0:T(8,128)(2,1)} %get-tuple-element.62), channel_id=1, source_target_pairs={{0,24},{1,97},{2,26},{3,99},{4,28},{5,101},{6,30},{7,103},{8,0},{9... | collective-permute-start | bytes 6193160 | tf_op jit(solution)/shard_map/ppermute | solution.py:351
  65.8 3.2 %collective-permute-done.2.refs_0_ = bf16[2,1440,128]{2,1,0:T(8,128)(2,1)} collective-permute-done((bf16[2,1440,128]{2,1,0:T(8,128)(2,1)}, bf16[2,1440,128]{2,1,0:T(8,128)(2,1)}, u32[]{:S(2)}, u32[]{:S(2)}) %collective-permute-start.2) | collective-permute-done | bytes 737312 | tf_op jit(solution)/shard_map/ppermute | solution.py:350
  69.0 0.0 collective-permute-done.3.refs_1_
  69.0 2.8 %add_far.3 = (bf16[4,1440,128]{2,1,0:T(8,128)(2,1)}, bf16[4,1440,128]{2,1,0:T(8,128)(2,1)}) custom-call(bf16[2,1440,128]{2,1,0:T(8,128)(2,1)} %collective-permute-done.2.refs_0_, bf16[2,1440,128]{2,1,0:T(8,128)(2,1)} %collective-permute-done.3.refs_1_, ...), custom_call_target="tpu_custom_call", output_to_operand_aliasing={{0}: (2, {}), {1}: (3, {})} | custom-call | tf_op jit(solution)/shard_map/add_far/pallas_call | solution.py:221
  71.7 0.8 collective-permute-start.4
  72.6 2.5 %collective-permute-start.5 = (bf16[4,1440,128]{2,1,0:T(8,128)(2,1)}, bf16[4,1440,128]{2,1,0:T(8,128)(2,1)}, u32[]{:S(2)}, u32[]{:S(2)}) collective-permute-start(bf16[4,1440,128]{2,1,0:T(8,128)(2,1)} %get-tuple-element.60), channel_id=1, source_target_pairs={{0,24},{1,97},{2,26},{3,99},{4,28},{5,101},{6,30},{7,103},{8,0},{9... | collective-permute-start | bytes 4423688 | tf_op jit(solution)/shard_map/ppermute | solution.py:351
  75.0 22.5 %back.1 = (bf16[384,6144]{1,0:T(8,128)(2,1)}, f32[8,128]{1,0:T(8,128)}) custom-call(s32[12,12]{1,0:T(8,128)} %refs_0_.1, s32[12,12]{1,0:T(8,128)} %refs_1_.1, bf16[384,1536]{1,0:T(8,128)(2,1)} %get-tuple-element.46.refs_2_, bf16[384,1536]{1,0:T(8,128)(2,1)} %get-tuple-element.47.refs_3_, bf16[12,12,128,128]{3,2,1,0:T(8,128)(2,1)} %refs_4_.1, ...), custom_call_target="tpu_custom_call" | custom-call | flops 24999999488 | bytes 16777216 | tf_op jit(solution)/shard_map/back/pallas_call | solution.py:186
  97.5 0.0 reduce-scatter.2.cloned.1.call-update
  97.6 0.0 collective-permute-done.7.refs_2_
  97.6 4.3 %add_near.2 = (bf16[1008,128]{1,0:T(8,128)(2,1)}, bf16[1008,128]{1,0:T(8,128)(2,1)}, bf16[2016,128]{1,0:T(8,128)(2,1)}, bf16[2016,128]{1,0:T(8,128)(2,1)}, bf16[2016,128]{1,0:T(8,128)(2,1)}) custom-call(bf16[4,2016,128]{2,1,0:T(8,128)(2,1)} %get-tuple-element.61.refs_0_, bf16[4,2016,128]{2,1,0:T(8,128)(2,1)} %collective-permute-done.6.refs_1_, ...), custom_call_target="tpu_custom_call" | custom-call | flops 199999995904 | tf_op jit(solution)/shard_map/add_near/pallas_call | solution.py:221
  101.9 2.1 %collective-permute-start.8 = (bf16[1008,128]{1,0:T(8,128)(2,1)}, bf16[1008,128]{1,0:T(8,128)(2,1)}, u32[]{:S(2)}, u32[]{:S(2)}) collective-permute-start(bf16[1008,128]{1,0:T(8,128)(2,1)} %get-tuple-element.64), channel_id=1, source_target_pairs={{0,32},{1,9},{2,34},{3,11},{4,36},{5,13},{6,38},{7,15},{8,40},{9,1... | collective-permute-start | bytes 774152 | tf_op jit(solution)/shard_map/ppermute | solution.py:350
  103.9 2.3 %collective-permute-start.9 = (bf16[1008,128]{1,0:T(8,128)(2,1)}, bf16[1008,128]{1,0:T(8,128)(2,1)}, u32[]{:S(2)}, u32[]{:S(2)}) collective-permute-start(bf16[1008,128]{1,0:T(8,128)(2,1)} %get-tuple-element.65), channel_id=1, source_target_pairs={{0,96},{1,25},{2,98},{3,27},{4,100},{5,29},{6,102},{7,31},{8,104},... | collective-permute-start | bytes 774152 | tf_op jit(solution)/shard_map/ppermute | solution.py:351
  106.2 4.4 %collective-permute-done.8.refs_0_ = bf16[1008,128]{1,0:T(8,128)(2,1)} collective-permute-done((bf16[1008,128]{1,0:T(8,128)(2,1)}, bf16[1008,128]{1,0:T(8,128)(2,1)}, u32[]{:S(2)}, u32[]{:S(2)}) %collective-permute-start.8) | collective-permute-done | bytes 258080 | tf_op jit(solution)/shard_map/ppermute | solution.py:350
  110.6 2.2 %add_far2.2 = (bf16[2016,128]{1,0:T(8,128)(2,1)}, bf16[2016,128]{1,0:T(8,128)(2,1)}) custom-call(bf16[1008,128]{1,0:T(8,128)(2,1)} %collective-permute-done.8.refs_0_, bf16[1008,128]{1,0:T(8,128)(2,1)} %collective-permute-done.9.refs_1_, bf16[2016,128]{1,0:T(8,128)(2,1)} %get-tuple-element.66.refs_2_, ...), custom_call_target="tpu_custom_call", output_to_operand_aliasing={{0}: (2, {}), {1}: (3, {})} | custom-call | tf_op jit(solution)/shard_map/add_far2/pallas_call | solution.py:221
  112.8 0.0 collective-permute-done.4.refs_1_
  112.8 0.0 collective-permute-done.5.refs_2_
  112.8 3.6 %add_near.3 = (bf16[720,128]{1,0:T(8,128)(2,1)}, bf16[720,128]{1,0:T(8,128)(2,1)}, bf16[1440,128]{1,0:T(8,128)(2,1)}, bf16[1440,128]{1,0:T(8,128)(2,1)}, bf16[1440,128]{1,0:T(8,128)(2,1)}) custom-call(bf16[4,1440,128]{2,1,0:T(8,128)(2,1)} %get-tuple-element.59.refs_0_, bf16[4,1440,128]{2,1,0:T(8,128)(2,1)} %collective-permute-done.4.refs_1_, ...), custom_call_target="tpu_custom_call" | custom-call | tf_op jit(solution)/shard_map/add_near/pallas_call | solution.py:221
  116.4 1.9 %collective-permute-start.10 = (bf16[720,128]{1,0:T(8,128)(2,1)}, bf16[720,128]{1,0:T(8,128)(2,1)}, u32[]{:S(2)}, u32[]{:S(2)}) collective-permute-start(bf16[720,128]{1,0:T(8,128)(2,1)} %get-tuple-element.70), channel_id=1, source_target_pairs={{0,32},{1,9},{2,34},{3,11},{4,36},{5,13},{6,38},{7,15},{8,40},{9,1... | collective-permute-start | bytes 552968 | tf_op jit(solution)/shard_map/ppermute | solution.py:350
  118.2 1.7 %collective-permute-start.11 = (bf16[720,128]{1,0:T(8,128)(2,1)}, bf16[720,128]{1,0:T(8,128)(2,1)}, u32[]{:S(2)}, u32[]{:S(2)}) collective-permute-start(bf16[720,128]{1,0:T(8,128)(2,1)} %get-tuple-element.71), channel_id=1, source_target_pairs={{0,96},{1,25},{2,98},{3,27},{4,100},{5,29},{6,102},{7,31},{8,104},... | collective-permute-start | bytes 552968 | tf_op jit(solution)/shard_map/ppermute | solution.py:351
  119.9 0.3 collective-permute-start.14
  120.3 2.9 %collective-permute-start.15 = (bf16[2016,128]{1,0:T(8,128)(2,1)}, bf16[2016,128]{1,0:T(8,128)(2,1)}, u32[]{:S(2)}, u32[]{:S(2)}) collective-permute-start(bf16[2016,128]{1,0:T(8,128)(2,1)} %get-tuple-element.77), channel_id=1, source_target_pairs={{0,96},{1,25},{2,98},{3,27},{4,100},{5,29},{6,102},{7,31},{8,104},... | collective-permute-start | bytes 1548296 | tf_op jit(solution)/shard_map/ppermute | solution.py:351
  123.2 0.5 collective-permute-done.10.refs_0_
  123.7 0.4 collective-permute-done.11.refs_1_
  124.1 2.0 %add_far2.3 = (bf16[1440,128]{1,0:T(8,128)(2,1)}, bf16[1440,128]{1,0:T(8,128)(2,1)}) custom-call(bf16[720,128]{1,0:T(8,128)(2,1)} %collective-permute-done.10.refs_0_, bf16[720,128]{1,0:T(8,128)(2,1)} %collective-permute-done.11.refs_1_, bf16[1440,128]{1,0:T(8,128)(2,1)} %get-tuple-element.72.refs_2_, ...), custom_call_target="tpu_custom_call", output_to_operand_aliasing={{0}: (2, {}), {1}: (3, {})} | custom-call | tf_op jit(solution)/shard_map/add_far2/pallas_call | solution.py:221
  126.1 1.6 %collective-permute-start.12 = (bf16[1440,128]{1,0:T(8,128)(2,1)}, bf16[1440,128]{1,0:T(8,128)(2,1)}, u32[]{:S(2)}, u32[]{:S(2)}) collective-permute-start(bf16[1440,128]{1,0:T(8,128)(2,1)} %get-tuple-element.74), channel_id=1, source_target_pairs={{0,32},{1,9},{2,34},{3,11},{4,36},{5,13},{6,38},{7,15},{8,40},{9,1... | collective-permute-start | bytes 1105928 | tf_op jit(solution)/shard_map/ppermute | solution.py:350
  127.7 1.6 %collective-permute-start.13 = (bf16[1440,128]{1,0:T(8,128)(2,1)}, bf16[1440,128]{1,0:T(8,128)(2,1)}, u32[]{:S(2)}, u32[]{:S(2)}) collective-permute-start(bf16[1440,128]{1,0:T(8,128)(2,1)} %get-tuple-element.75), channel_id=1, source_target_pairs={{0,96},{1,25},{2,98},{3,27},{4,100},{5,29},{6,102},{7,31},{8,104},... | collective-permute-start | bytes 1105928 | tf_op jit(solution)/shard_map/ppermute | solution.py:351
  129.4 1.2 collective-permute-done.14.got_p
  130.6 0.0 collective-permute-done.15.got_m
  130.6 2.4 %add_last.2 = (f32[12,96,128]{2,1,0:T(8,128)}, f32[12,96,128]{2,1,0:T(8,128)}, f32[12,96,128]{2,1,0:T(8,128)}) custom-call(bf16[2016,128]{1,0:T(8,128)(2,1)} %get-tuple-element.76.kept, bf16[2016,128]{1,0:T(8,128)(2,1)} %collective-permute-done.14.got_p, bf16[2016,128]{1,0:T(8,128)(2,1)} %collective-permute-done.15.got_m), custom_call_target="tpu_custom_call" | custom-call | tf_op jit(solution)/shard_map/add_last/pallas_call | solution.py:308
  133.0 2.2 %collective-permute-done.12.got_p = bf16[1440,128]{1,0:T(8,128)(2,1)} collective-permute-done((bf16[1440,128]{1,0:T(8,128)(2,1)}, bf16[1440,128]{1,0:T(8,128)(2,1)}, u32[]{:S(2)}, u32[]{:S(2)}) %collective-permute-start.12) | collective-permute-done | bytes 368672 | tf_op jit(solution)/shard_map/ppermute | solution.py:350
  135.2 0.4 collective-permute-done.13.got_m
  135.5 2.2 %add_last.3 = (f32[12,96,128]{2,1,0:T(8,128)}, f32[12,96,128]{2,1,0:T(8,128)}, f32[12,96,128]{2,1,0:T(8,128)}) custom-call(bf16[1440,128]{1,0:T(8,128)(2,1)} %get-tuple-element.69.kept, bf16[1440,128]{1,0:T(8,128)(2,1)} %collective-permute-done.12.got_p, ...), custom_call_target="tpu_custom_call", output_to_operand_aliasing={{0}: (3, {}), {1}: (4, {}), {2}: (5, {})} | custom-call | tf_op jit(solution)/shard_map/add_last/pallas_call | solution.py:308
  137.7 0.8 reduce-scatter.2.cloned.1.call-done
  (5 shorter events, 0.0 us)
Async XLA Ops:
  7.2 131.3 %reduce-scatter.2.cloned.1.call-start = ((), (), s32[]{:S(2)}) async-start(), calls=%async_computation.1 | async-start | bytes 5308416 | tf_op jit(solution)/shard_map/reduce_scatter | solution.py:388
  7.3 0.7 copy-start
  8.0 0.7 copy-start.1
  8.7 0.7 copy-start.2
  33.6 25.7 %collective-permute-start = (bf16[2,2016,128]{2,1,0:T(8,128)(2,1)}, bf16[2,2016,128]{2,1,0:T(8,128)(2,1)}, u32[]{:S(2)}, u32[]{:S(2)}) collective-permute-start(bf16[2,2016,128]{2,1,0:T(8,128)(2,1)} %get-tuple-element.48), channel_id=1, source_target_pairs={{0,8},{1,33},{2,10},{3,35},{4,12},{5,37},{6,14},{7,39},{8,16},{9,4... | collective-permute-start | bytes 3096584 | tf_op jit(solution)/shard_map/ppermute | solution.py:350
  35.3 23.9 %collective-permute-start.1 = (bf16[2,2016,128]{2,1,0:T(8,128)(2,1)}, bf16[2,2016,128]{2,1,0:T(8,128)(2,1)}, u32[]{:S(2)}, u32[]{:S(2)}) collective-permute-start(bf16[2,2016,128]{2,1,0:T(8,128)(2,1)} %get-tuple-element.49), channel_id=1, source_target_pairs={{0,24},{1,97},{2,26},{3,99},{4,28},{5,101},{6,30},{7,103},{8,0},{9... | collective-permute-start | bytes 3096584 | tf_op jit(solution)/shard_map/ppermute | solution.py:351
  55.9 13.0 %collective-permute-start.2 = (bf16[2,1440,128]{2,1,0:T(8,128)(2,1)}, bf16[2,1440,128]{2,1,0:T(8,128)(2,1)}, u32[]{:S(2)}, u32[]{:S(2)}) collective-permute-start(bf16[2,1440,128]{2,1,0:T(8,128)(2,1)} %get-tuple-element.52.refs_4_), channel_id=1, source_target_pairs={{0,8},{1,33},{2,10},{3,35},{4,12},{5,37},{6,14},{7,39},{8,16},{9,4... | collective-permute-start | bytes 2211848 | tf_op jit(solution)/shard_map/ppermute | solution.py:350
  56.5 12.5 %collective-permute-start.3 = (bf16[2,1440,128]{2,1,0:T(8,128)(2,1)}, bf16[2,1440,128]{2,1,0:T(8,128)(2,1)}, u32[]{:S(2)}, u32[]{:S(2)}) collective-permute-start(bf16[2,1440,128]{2,1,0:T(8,128)(2,1)} %get-tuple-element.54), channel_id=1, source_target_pairs={{0,24},{1,97},{2,26},{3,99},{4,28},{5,101},{6,30},{7,103},{8,0},{9... | collective-permute-start | bytes 2211848 | tf_op jit(solution)/shard_map/ppermute | solution.py:351
  62.5 35.0 %collective-permute-start.6 = (bf16[4,2016,128]{2,1,0:T(8,128)(2,1)}, bf16[4,2016,128]{2,1,0:T(8,128)(2,1)}, u32[]{:S(2)}, u32[]{:S(2)}) collective-permute-start(bf16[4,2016,128]{2,1,0:T(8,128)(2,1)} %get-tuple-element.53.refs_4_.refs_6_), channel_id=1, source_target_pairs={{0,8},{1,33},{2,10},{3,35},{4,12},{5,37},{6,14},{7,39},{8,16},{9,4... | collective-permute-start | bytes 6193160 | tf_op jit(solution)/shard_map/ppermute | solution.py:350
  62.5 35.0 %collective-permute-start.7 = (bf16[4,2016,128]{2,1,0:T(8,128)(2,1)}, bf16[4,2016,128]{2,1,0:T(8,128)(2,1)}, u32[]{:S(2)}, u32[]{:S(2)}) collective-permute-start(bf16[4,2016,128]{2,1,0:T(8,128)(2,1)} %get-tuple-element.62), channel_id=1, source_target_pairs={{0,24},{1,97},{2,26},{3,99},{4,28},{5,101},{6,30},{7,103},{8,0},{9... | collective-permute-start | bytes 6193160 | tf_op jit(solution)/shard_map/ppermute | solution.py:351
  71.7 41.1 %collective-permute-start.4 = (bf16[4,1440,128]{2,1,0:T(8,128)(2,1)}, bf16[4,1440,128]{2,1,0:T(8,128)(2,1)}, u32[]{:S(2)}, u32[]{:S(2)}) collective-permute-start(bf16[4,1440,128]{2,1,0:T(8,128)(2,1)} %get-tuple-element.57.refs_7_), channel_id=1, source_target_pairs={{0,8},{1,33},{2,10},{3,35},{4,12},{5,37},{6,14},{7,39},{8,16},{9,4... | collective-permute-start | bytes 4423688 | tf_op jit(solution)/shard_map/ppermute | solution.py:350
  72.6 40.2 %collective-permute-start.5 = (bf16[4,1440,128]{2,1,0:T(8,128)(2,1)}, bf16[4,1440,128]{2,1,0:T(8,128)(2,1)}, u32[]{:S(2)}, u32[]{:S(2)}) collective-permute-start(bf16[4,1440,128]{2,1,0:T(8,128)(2,1)} %get-tuple-element.60), channel_id=1, source_target_pairs={{0,24},{1,97},{2,26},{3,99},{4,28},{5,101},{6,30},{7,103},{8,0},{9... | collective-permute-start | bytes 4423688 | tf_op jit(solution)/shard_map/ppermute | solution.py:351
  101.9 8.8 %collective-permute-start.8 = (bf16[1008,128]{1,0:T(8,128)(2,1)}, bf16[1008,128]{1,0:T(8,128)(2,1)}, u32[]{:S(2)}, u32[]{:S(2)}) collective-permute-start(bf16[1008,128]{1,0:T(8,128)(2,1)} %get-tuple-element.64), channel_id=1, source_target_pairs={{0,32},{1,9},{2,34},{3,11},{4,36},{5,13},{6,38},{7,15},{8,40},{9,1... | collective-permute-start | bytes 774152 | tf_op jit(solution)/shard_map/ppermute | solution.py:350
  103.9 6.7 %collective-permute-start.9 = (bf16[1008,128]{1,0:T(8,128)(2,1)}, bf16[1008,128]{1,0:T(8,128)(2,1)}, u32[]{:S(2)}, u32[]{:S(2)}) collective-permute-start(bf16[1008,128]{1,0:T(8,128)(2,1)} %get-tuple-element.65), channel_id=1, source_target_pairs={{0,96},{1,25},{2,98},{3,27},{4,100},{5,29},{6,102},{7,31},{8,104},... | collective-permute-start | bytes 774152 | tf_op jit(solution)/shard_map/ppermute | solution.py:351
  116.4 7.3 %collective-permute-start.10 = (bf16[720,128]{1,0:T(8,128)(2,1)}, bf16[720,128]{1,0:T(8,128)(2,1)}, u32[]{:S(2)}, u32[]{:S(2)}) collective-permute-start(bf16[720,128]{1,0:T(8,128)(2,1)} %get-tuple-element.70), channel_id=1, source_target_pairs={{0,32},{1,9},{2,34},{3,11},{4,36},{5,13},{6,38},{7,15},{8,40},{9,1... | collective-permute-start | bytes 552968 | tf_op jit(solution)/shard_map/ppermute | solution.py:350
  118.2 5.9 %collective-permute-start.11 = (bf16[720,128]{1,0:T(8,128)(2,1)}, bf16[720,128]{1,0:T(8,128)(2,1)}, u32[]{:S(2)}, u32[]{:S(2)}) collective-permute-start(bf16[720,128]{1,0:T(8,128)(2,1)} %get-tuple-element.71), channel_id=1, source_target_pairs={{0,96},{1,25},{2,98},{3,27},{4,100},{5,29},{6,102},{7,31},{8,104},... | collective-permute-start | bytes 552968 | tf_op jit(solution)/shard_map/ppermute | solution.py:351
  119.9 10.6 %collective-permute-start.14 = (bf16[2016,128]{1,0:T(8,128)(2,1)}, bf16[2016,128]{1,0:T(8,128)(2,1)}, u32[]{:S(2)}, u32[]{:S(2)}) collective-permute-start(bf16[2016,128]{1,0:T(8,128)(2,1)} %get-tuple-element.68.refs_3_), channel_id=1, source_target_pairs={{0,32},{1,9},{2,34},{3,11},{4,36},{5,13},{6,38},{7,15},{8,40},{9,1... | collective-permute-start | bytes 1548296 | tf_op jit(solution)/shard_map/ppermute | solution.py:350
  120.3 10.3 %collective-permute-start.15 = (bf16[2016,128]{1,0:T(8,128)(2,1)}, bf16[2016,128]{1,0:T(8,128)(2,1)}, u32[]{:S(2)}, u32[]{:S(2)}) collective-permute-start(bf16[2016,128]{1,0:T(8,128)(2,1)} %get-tuple-element.77), channel_id=1, source_target_pairs={{0,96},{1,25},{2,98},{3,27},{4,100},{5,29},{6,102},{7,31},{8,104},... | collective-permute-start | bytes 1548296 | tf_op jit(solution)/shard_map/ppermute | solution.py:351
  126.1 9.0 %collective-permute-start.12 = (bf16[1440,128]{1,0:T(8,128)(2,1)}, bf16[1440,128]{1,0:T(8,128)(2,1)}, u32[]{:S(2)}, u32[]{:S(2)}) collective-permute-start(bf16[1440,128]{1,0:T(8,128)(2,1)} %get-tuple-element.74), channel_id=1, source_target_pairs={{0,32},{1,9},{2,34},{3,11},{4,36},{5,13},{6,38},{7,15},{8,40},{9,1... | collective-permute-start | bytes 1105928 | tf_op jit(solution)/shard_map/ppermute | solution.py:350
  127.7 7.8 %collective-permute-start.13 = (bf16[1440,128]{1,0:T(8,128)(2,1)}, bf16[1440,128]{1,0:T(8,128)(2,1)}, u32[]{:S(2)}, u32[]{:S(2)}) collective-permute-start(bf16[1440,128]{1,0:T(8,128)(2,1)} %get-tuple-element.75), channel_id=1, source_target_pairs={{0,96},{1,25},{2,98},{3,27},{4,100},{5,29},{6,102},{7,31},{8,104},... | collective-permute-start | bytes 1105928 | tf_op jit(solution)/shard_map/ppermute | solution.py:351
Sparse Core Ops, SparseCore 0:
  97.7 40.7 reduce-scatter.1
